TPU v7x, 32 devices: a whole 2x2x4 slice. The times are simulated.
32 devices in a mesh: shot: 8 (over z, y), gx: 4 (over x, core).
Axes of the slice: x: 2, y: 2, z: 4, core: 2. Of those that a mesh axis runs over, the one named last changes fastest.
Arguments:
- source_prev: float32 [8, 64, 64, 128], P('shot', 'gx'), may hold values from -6 to 6
- source_now: float32 [8, 64, 64, 128], P('shot', 'gx'), may hold values from -6 to 6
- receiver_prev: float32 [8, 64, 64, 128], P('shot', 'gx'), may hold values from -6 to 6
- receiver_now: float32 [8, 64, 64, 128], P('shot', 'gx'), may hold values from -6 to 6
- courant: float32 [64, 64, 128], P('gx'), may hold values from 0.05 to 0.3
- source_cells: int32 [8, 8], P('shot'), may hold values from 0 to 524287
- wavelet: float32 [8, 2, 8], P('shot'), may hold values from -128 to 128
- receiver_cells: int32 [8, 512], P('shot'), may hold values from 0 to 524287
- receiver_data: float32 [8, 2, 512], P('shot'), may hold values from -128 to 128
- offsets: int32 [9], replicated, may hold values from -8 to 8, as said below
- conv_weight: float32 [64, 9, 3, 3, 3], replicated, may hold values from -1.25 to 1.25
- conv_bias: float32 [64], replicated, may hold values from -3 to 3
Outputs:
- summary: float32 [64, 16, 512], P(None, 'gx', 'shot')
Inputs may be any that keep to these rules, and one draw needn't show every extreme that they name: The offsets are distinct and include -8 and 8.
All inputs are finite; a program needn't handle non-finite values.
Results may differ from a plain program's by a relative error of at most 0.0003.
Values sent between devices are 32-bit elements; how exact they have to be, the bound alone decides.
A program may use at most 64 MiB of HBM per device.

v0:
```python
import jax
import jax.numpy as jnp
from jax import lax
from jax.sharding import PartitionSpec as P

HMAX = 8


def padded_2(block, sides, width):
    for axis, dim in sides:
        count = lax.axis_size(axis)
        forward = [(i, i + 1) for i in range(count - 1)]
        backward = [(target, source) for source, target in forward]
        low = lax.ppermute(
            lax.slice_in_dim(block, block.shape[dim] - width, None, axis=dim), axis, forward
        )
        high = lax.ppermute(lax.slice_in_dim(block, 0, width, axis=dim), axis, backward)
        block = jnp.concatenate([low, block, high], axis=dim)
    return block


def inject(cells_here, first_x, cell_index, amplitudes, size_y, size_z):
    plane_size = size_y * size_z
    column = cell_index // plane_size
    within = cell_index % plane_size
    local_x = column - first_x
    inside = (local_x >= 0) & (local_x < cells_here)
    target = jnp.where(inside, local_x * plane_size + within, cells_here * plane_size)
    flat_cells = jnp.zeros((cells_here * plane_size + 1,), jnp.float32).at[target].add(amplitudes)
    return flat_cells[:-1].reshape(cells_here, size_y, size_z)


def laplace_step(previous, extended, courant, sources):
    center = extended[:, 1:-1]
    padded = jnp.pad(center, ((0, 0), (0, 0), (1, 1), (1, 1)))
    laplace = extended[:, 2:] + extended[:, :-2]
    laplace = laplace + padded[:, :, 2:, 1:-1] + padded[:, :, :-2, 1:-1]
    laplace = laplace + padded[:, :, 1:-1, 2:] + padded[:, :, 1:-1, :-2] - 6.0 * center
    return 2.0 * center - previous + courant * laplace + sources


def coarsen(image_block):
    size_x, size_y, size_z = image_block.shape
    return image_block.reshape(size_x // 4, 4, size_y // 4, 4, size_z // 4, 4).mean(axis=(1, 3, 5))


def offset_image(wide, offsets, margin, cells_x):

    def per_offset(offset_value):
        forward_part = lax.dynamic_slice_in_dim(wide, margin + offset_value, cells_x, 1)
        backward_part = lax.dynamic_slice_in_dim(wide, margin - offset_value, cells_x, 1)
        image_block = forward_part[0] * backward_part[1] + forward_part[2] * backward_part[3]
        return coarsen(image_block)

    return lax.map(per_offset, offsets)


def conv_apply(padded, conv_weight, conv_bias):
    channels, span_x, span_y, span_z = padded.shape
    size_x, size_y, size_z = (span_x - 2, span_y - 2, span_z - 2)
    patches = jnp.stack(
        [
            padded[:, step_x : step_x + size_x, step_y : step_y + size_y, step_z : step_z + size_z]
            for step_x in range(3)
            for step_y in range(3)
            for step_z in range(3)
        ],
        axis=1,
    )
    patches = patches.reshape(channels * 27, size_x * size_y * size_z)
    matrix = conv_weight.reshape(conv_weight.shape[0], channels * 27)
    result = jnp.dot(
        matrix, patches, precision=lax.Precision.HIGHEST, preferred_element_type=jnp.float32
    )
    result = result + conv_bias[:, None]
    return result.reshape(conv_weight.shape[0], size_x, size_y * size_z)


def local(
    source_prev,
    source_now,
    receiver_prev,
    receiver_now,
    courant,
    source_cells,
    wavelet,
    receiver_cells,
    receiver_data,
    offsets,
    conv_weight,
    conv_bias,
):
    cells_x, size_y, size_z = courant.shape
    slab_index = lax.axis_index("gx")
    grid_x = cells_x * lax.axis_size("gx")

    def sources_at(step_index, cells_here, first_x):
        return jnp.stack(
            [
                inject(
                    cells_here, first_x, source_cells[0], wavelet[0, step_index], size_y, size_z
                ),
                inject(
                    cells_here,
                    first_x,
                    receiver_cells[0],
                    receiver_data[0, step_index],
                    size_y,
                    size_z,
                ),
            ]
        )

    depth = HMAX + 2
    packed = jnp.stack([source_prev[0], receiver_prev[0], source_now[0], receiver_now[0], courant])
    extended = padded_2(packed, (("gx", 1),), depth)

    def inside_grid(margin):
        column = slab_index * cells_x - margin + jnp.arange(cells_x + 2 * margin, dtype=jnp.int32)
        return ((column >= 0) & (column < grid_x)).astype(jnp.float32)[:, None, None]

    first_margin = depth - 1
    second_margin = depth - 2
    first_level = laplace_step(
        extended[0:2, 1:-1],
        extended[2:4],
        extended[4, 1:-1],
        sources_at(0, cells_x + 2 * first_margin, slab_index * cells_x - first_margin),
    )
    first_level = first_level * inside_grid(first_margin)
    second_level = laplace_step(
        extended[2:4, 2:-2],
        first_level,
        extended[4, 2:-2],
        sources_at(1, cells_x + 2 * second_margin, slab_index * cells_x - second_margin),
    )
    second_level = second_level * inside_grid(second_margin)
    wide = jnp.concatenate([first_level[:, 1:-1], second_level], axis=0)
    coarse = offset_image(wide, offsets, HMAX, cells_x)
    summed = lax.psum(coarse, "shot")
    rimmed = padded_2(summed, (("gx", 1),), 1)
    row_count = summed.shape[2] // lax.axis_size("shot")
    padded = jnp.pad(rimmed, ((0, 0), (0, 0), (1, 1), (1, 1)))
    window = lax.dynamic_slice_in_dim(padded, lax.axis_index("shot") * row_count, row_count + 2, 2)
    return conv_apply(window, conv_weight, conv_bias)


def solution(mesh):
    in_specs = (
        P("shot", "gx", None, None),
        P("shot", "gx", None, None),
        P("shot", "gx", None, None),
        P("shot", "gx", None, None),
        P("gx", None, None),
        P("shot", None),
        P("shot", None, None),
        P("shot", None),
        P("shot", None, None),
        P(),
        P(),
        P(),
    )
    out_specs = P(None, "gx", "shot")
    return jax.shard_map(local, mesh=mesh, in_specs=in_specs, out_specs=out_specs, check_vma=False)
```

profile of v0, /device:TPU:25, one launch (start us, length us, event | category | flops | bytes accessed | tf_op | source)
XLA Modules:
  0.0 423.8 jit_solution(12319107540429221168)
XLA Ops:
  16.9 4.3 %scatter_custom_fusion.1 = f32[278529]{0:T(1024)} fusion(s32[512]{0:T(512)S(1)} %bitcast.185, f32[512]{0:T(512)S(1)} %bitcast.187, f32[]{:T(128)} %constant.140.clone.1), kind=kCustom, calls=%fused_computation.49 | custom fusion | flops 512 | bytes 1114120 | tf_op jit(solution)/shard_map/scatter-add | solution.py:29
  28.9 4.3 %collective-permute-done = f32[5,10,64,128]{3,2,1,0:T(8,128)} collective-permute-done((f32[5,10,64,128]{3,2,1,0:T(8,128)}, f32[5,10,64,128]{3,2,1,0:T(8,128)}, u32[]{:S(2)}, u32[]{:S(2)}) %collective-permute-start) | collective-permute-done | bytes 1638432 | tf_op jit(solution)/shard_map/ppermute | solution.py:14
  33.3 4.4 %collective-permute-done.1 = f32[5,10,64,128]{3,2,1,0:T(8,128)} collective-permute-done((f32[5,10,64,128]{3,2,1,0:T(8,128)}, f32[5,10,64,128]{3,2,1,0:T(8,128)}, u32[]{:S(2)}, u32[]{:S(2)}) %collective-permute-start.1) | collective-permute-done | bytes 1638432 | tf_op jit(solution)/shard_map/ppermute | solution.py:17
  50.7 280.1 %while.13 = (s32[]{:T(128)}, f32[9,4,16,32]{3,2,1,0:T(8,128)}, s32[9]{0:T(128)S(1)}, f32[4,32,64,128]{3,2,1,0:T(8,128)}, s32[]{:T(128)}, /*index=5*/s32[]{:T(128...) while((s32[]{:T(128)}, f32[9,4,16,32]{3,2,1,0:T(8,128)}, s32[9]{0:T(128)S(1)}, ...), condition=%wide.region_6.7_spmd, body=%wide.region_4.6_spmd.sunk | while | flops 524301 | bytes 4244249 | solution.py:55
  55.5 18.6 %add.537 = f32[4,4,16,4,32,4]{5,4,3,2,1,0:T(8,128)} reshape(f32[1,16,64,128]{3,2,1,0:T(8,128)S(1)} %fusion.51) | data formatting | bytes 1048576 | tf_op jit(solution)/shard_map/while/body/eval_jaxpr/add | solution.py:52
  74.2 7.1 %reduce_sum.14 = f32[4,16,32]{2,1,0:T(8,128)S(1)} reduce(f32[4,4,16,4,32,4]{5,4,3,2,1,0:T(8,128)} %add.537, f32[]{:T(128)} %constant.140.clone.1..sunk), dimensions={1,3,5}, to_apply=%region_5.5 | reduce | flops 129024 | bytes 532484 | tf_op jit(solution)/shard_map/while/body/eval_jaxpr/reduce_sum | solution.py:44
  86.6 18.6 %add.537 = f32[4,4,16,4,32,4]{5,4,3,2,1,0:T(8,128)} reshape(f32[1,16,64,128]{3,2,1,0:T(8,128)S(1)} %fusion.51) | data formatting | bytes 1048576 | tf_op jit(solution)/shard_map/while/body/eval_jaxpr/add | solution.py:52
  105.3 7.1 %reduce_sum.14 = f32[4,16,32]{2,1,0:T(8,128)S(1)} reduce(f32[4,4,16,4,32,4]{5,4,3,2,1,0:T(8,128)} %add.537, f32[]{:T(128)} %constant.140.clone.1..sunk), dimensions={1,3,5}, to_apply=%region_5.5 | reduce | flops 129024 | bytes 532484 | tf_op jit(solution)/shard_map/while/body/eval_jaxpr/reduce_sum | solution.py:44
  117.8 18.6 %add.537 = f32[4,4,16,4,32,4]{5,4,3,2,1,0:T(8,128)} reshape(f32[1,16,64,128]{3,2,1,0:T(8,128)S(1)} %fusion.51) | data formatting | bytes 1048576 | tf_op jit(solution)/shard_map/while/body/eval_jaxpr/add | solution.py:52
  136.4 7.1 %reduce_sum.14 = f32[4,16,32]{2,1,0:T(8,128)S(1)} reduce(f32[4,4,16,4,32,4]{5,4,3,2,1,0:T(8,128)} %add.537, f32[]{:T(128)} %constant.140.clone.1..sunk), dimensions={1,3,5}, to_apply=%region_5.5 | reduce | flops 129024 | bytes 532484 | tf_op jit(solution)/shard_map/while/body/eval_jaxpr/reduce_sum | solution.py:44
  148.9 18.6 %add.537 = f32[4,4,16,4,32,4]{5,4,3,2,1,0:T(8,128)} reshape(f32[1,16,64,128]{3,2,1,0:T(8,128)S(1)} %fusion.51) | data formatting | bytes 1048576 | tf_op jit(solution)/shard_map/while/body/eval_jaxpr/add | solution.py:52
  167.5 7.1 %reduce_sum.14 = f32[4,16,32]{2,1,0:T(8,128)S(1)} reduce(f32[4,4,16,4,32,4]{5,4,3,2,1,0:T(8,128)} %add.537, f32[]{:T(128)} %constant.140.clone.1..sunk), dimensions={1,3,5}, to_apply=%region_5.5 | reduce | flops 129024 | bytes 532484 | tf_op jit(solution)/shard_map/while/body/eval_jaxpr/reduce_sum | solution.py:44
  180.0 18.6 %add.537 = f32[4,4,16,4,32,4]{5,4,3,2,1,0:T(8,128)} reshape(f32[1,16,64,128]{3,2,1,0:T(8,128)S(1)} %fusion.51) | data formatting | bytes 1048576 | tf_op jit(solution)/shard_map/while/body/eval_jaxpr/add | solution.py:52
  198.6 7.1 %reduce_sum.14 = f32[4,16,32]{2,1,0:T(8,128)S(1)} reduce(f32[4,4,16,4,32,4]{5,4,3,2,1,0:T(8,128)} %add.537, f32[]{:T(128)} %constant.140.clone.1..sunk), dimensions={1,3,5}, to_apply=%region_5.5 | reduce | flops 129024 | bytes 532484 | tf_op jit(solution)/shard_map/while/body/eval_jaxpr/reduce_sum | solution.py:44
  211.1 18.6 %add.537 = f32[4,4,16,4,32,4]{5,4,3,2,1,0:T(8,128)} reshape(f32[1,16,64,128]{3,2,1,0:T(8,128)S(1)} %fusion.51) | data formatting | bytes 1048576 | tf_op jit(solution)/shard_map/while/body/eval_jaxpr/add | solution.py:52
  229.8 7.1 %reduce_sum.14 = f32[4,16,32]{2,1,0:T(8,128)S(1)} reduce(f32[4,4,16,4,32,4]{5,4,3,2,1,0:T(8,128)} %add.537, f32[]{:T(128)} %constant.140.clone.1..sunk), dimensions={1,3,5}, to_apply=%region_5.5 | reduce | flops 129024 | bytes 532484 | tf_op jit(solution)/shard_map/while/body/eval_jaxpr/reduce_sum | solution.py:44
  242.2 18.6 %add.537 = f32[4,4,16,4,32,4]{5,4,3,2,1,0:T(8,128)} reshape(f32[1,16,64,128]{3,2,1,0:T(8,128)S(1)} %fusion.51) | data formatting | bytes 1048576 | tf_op jit(solution)/shard_map/while/body/eval_jaxpr/add | solution.py:52
  260.9 7.1 %reduce_sum.14 = f32[4,16,32]{2,1,0:T(8,128)S(1)} reduce(f32[4,4,16,4,32,4]{5,4,3,2,1,0:T(8,128)} %add.537, f32[]{:T(128)} %constant.140.clone.1..sunk), dimensions={1,3,5}, to_apply=%region_5.5 | reduce | flops 129024 | bytes 532484 | tf_op jit(solution)/shard_map/while/body/eval_jaxpr/reduce_sum | solution.py:44
  273.4 18.6 %add.537 = f32[4,4,16,4,32,4]{5,4,3,2,1,0:T(8,128)} reshape(f32[1,16,64,128]{3,2,1,0:T(8,128)S(1)} %fusion.51) | data formatting | bytes 1048576 | tf_op jit(solution)/shard_map/while/body/eval_jaxpr/add | solution.py:52
  292.0 7.1 %reduce_sum.14 = f32[4,16,32]{2,1,0:T(8,128)S(1)} reduce(f32[4,4,16,4,32,4]{5,4,3,2,1,0:T(8,128)} %add.537, f32[]{:T(128)} %constant.140.clone.1..sunk), dimensions={1,3,5}, to_apply=%region_5.5 | reduce | flops 129024 | bytes 532484 | tf_op jit(solution)/shard_map/while/body/eval_jaxpr/reduce_sum | solution.py:44
  304.5 18.6 %add.537 = f32[4,4,16,4,32,4]{5,4,3,2,1,0:T(8,128)} reshape(f32[1,16,64,128]{3,2,1,0:T(8,128)S(1)} %fusion.51) | data formatting | bytes 1048576 | tf_op jit(solution)/shard_map/while/body/eval_jaxpr/add | solution.py:52
  323.1 7.1 %reduce_sum.14 = f32[4,16,32]{2,1,0:T(8,128)S(1)} reduce(f32[4,4,16,4,32,4]{5,4,3,2,1,0:T(8,128)} %add.537, f32[]{:T(128)} %constant.140.clone.1..sunk), dimensions={1,3,5}, to_apply=%region_5.5 | reduce | flops 129024 | bytes 532484 | tf_op jit(solution)/shard_map/while/body/eval_jaxpr/reduce_sum | solution.py:44
  330.8 67.5 %all-reduce.5.cloned.1.call-done = f32[9,4,16,32]{3,2,1,0:T(8,128)} async-done(((f32[9,4,16,32]{3,2,1,0:T(8,128)}), f32[9,4,16,32]{3,2,1,0:T(8,128)}) %all-reduce.5.cloned.1.call-update) | async-done | bytes 73744 | tf_op jit(solution)/shard_map/psum | solution.py:140
  399.2 5.7 %collective-permute-start.2 = (f32[9,1,16,32]{3,2,1,0:T(8,128)S(1)}, f32[9,1,16,32]{3,2,1,0:T(8,128)S(1)}, u32[]{:S(2)}, u32[]{:S(2)}) collective-permute-start(f32[9,1,16,32]{3,2,1,0:T(8,128)S(1)} %get-tuple-element.90), channel_id=1, source_target_pairs={{0,1},{1,2},{2,3},{4,5},{5,6},{6,7},{8,9},{9,10},{10,11},{12,13},{... | collective-permute-start | bytes 55304 | tf_op jit(solution)/shard_map/ppermute | solution.py:14
  (123 shorter events, 70.0 us)
Async XLA Ops:
  6.5 2.3 copy-start
  6.5 391.7 %all-reduce.5.cloned.1.call-start = ((), (), s32[]{:S(2)}) async-start(), calls=%async_computation | async-start | bytes 589824 | tf_op jit(solution)/shard_map/psum | solution.py:140
  6.5 2.3 copy-start.1
  6.5 2.4 copy-start.2
  9.0 7.9 %copy-start.5 = (s32[1,512]{1,0:T(1,128)S(1)}, s32[1,512]{1,0:T(1,128)}, u32[]{:S(2)}) copy-start(s32[1,512]{1,0:T(1,128)} %param.21) | copy-start | bytes 6148
  9.0 7.9 %copy-start.4 = (f32[1,2,512]{2,1,0:T(2,128)S(1)}, f32[1,2,512]{2,1,0:T(2,128)}, u32[]{:S(2)}) copy-start(f32[1,2,512]{2,1,0:T(2,128)} %param.22) | copy-start | bytes 12292
  11.1 10.1 %copy-start.7 = (s32[1,8]{1,0:T(1,128)S(1)}, s32[1,8]{1,0:T(1,128)}, u32[]{:S(2)}) copy-start(s32[1,8]{1,0:T(1,128)} %param.19) | copy-start | bytes 100
  11.1 10.2 %copy-start.6 = (f32[1,2,8]{2,1,0:T(2,128)S(1)}, f32[1,2,8]{2,1,0:T(2,128)}, u32[]{:S(2)}) copy-start(f32[1,2,8]{2,1,0:T(2,128)} %param.20) | copy-start | bytes 196
  11.1 22.2 %collective-permute-start = (f32[5,10,64,128]{3,2,1,0:T(8,128)}, f32[5,10,64,128]{3,2,1,0:T(8,128)}, u32[]{:S(2)}, u32[]{:S(2)}) collective-permute-start(f32[5,10,64,128]{3,2,1,0:T(8,128)} %get-tuple-element.87), channel_id=1, source_target_pairs={{0,1},{1,2},{2,3},{4,5},{5,6},{6,7},{8,9},{9,10},{10,11},{12,13},{... | collective-permute-start | bytes 4915208 | tf_op jit(solution)/shard_map/ppermute | solution.py:14
  14.9 22.8 %collective-permute-start.1 = (f32[5,10,64,128]{3,2,1,0:T(8,128)}, f32[5,10,64,128]{3,2,1,0:T(8,128)}, u32[]{:S(2)}, u32[]{:S(2)}) collective-permute-start(f32[5,10,64,128]{3,2,1,0:T(8,128)} %get-tuple-element.88), channel_id=1, source_target_pairs={{1,0},{2,1},{3,2},{5,4},{6,5},{7,6},{9,8},{10,9},{11,10},{13,12},{... | collective-permute-start | bytes 4915208 | tf_op jit(solution)/shard_map/ppermute | solution.py:17
  40.4 1.3 slice-start
  40.4 1.6 slice-start.1
  44.5 1.2 slice-start.2
  44.5 1.5 slice-start.3
  48.4 2.3 copy-start.9
  50.7 356.4 %copy-start.3 = (f32[64,9,3,3,3]{0,4,3,2,1:T(4,128)S(1)}, f32[64,9,3,3,3]{0,4,3,2,1:T(4,128)}, u32[]{:S(2)}) copy-start(f32[64,9,3,3,3]{0,4,3,2,1:T(4,128)} %param.24) | copy-start | bytes 186628
  399.2 8.0 %collective-permute-start.2 = (f32[9,1,16,32]{3,2,1,0:T(8,128)S(1)}, f32[9,1,16,32]{3,2,1,0:T(8,128)S(1)}, u32[]{:S(2)}, u32[]{:S(2)}) collective-permute-start(f32[9,1,16,32]{3,2,1,0:T(8,128)S(1)} %get-tuple-element.90), channel_id=1, source_target_pairs={{0,1},{1,2},{2,3},{4,5},{5,6},{6,7},{8,9},{9,10},{10,11},{12,13},{... | collective-permute-start | bytes 55304 | tf_op jit(solution)/shard_map/ppermute | solution.py:14
  404.9 5.7 %collective-permute-start.3 = (f32[9,1,16,32]{3,2,1,0:T(8,128)S(1)}, f32[9,1,16,32]{3,2,1,0:T(8,128)S(1)}, u32[]{:S(2)}, u32[]{:S(2)}) collective-permute-start(f32[9,1,16,32]{3,2,1,0:T(8,128)S(1)} %get-tuple-element.89), channel_id=1, source_target_pairs={{1,0},{2,1},{3,2},{5,4},{6,5},{7,6},{9,8},{10,9},{11,10},{13,12},{... | collective-permute-start | bytes 55304 | tf_op jit(solution)/shard_map/ppermute | solution.py:17
  413.1 2.8 copy-start.8
Sparse Core Ops, SparseCore 0:
  330.9 67.2 all-reduce.4
where the time goes:
time: 427 us; the launch traced here: 424 us
  local copies, waits for them, and re-layouts  187 us (44%)
  other arithmetic  107 us (25%)
  waiting for transfers between devices  79.6 us (19%)
  loops' own time  22.5 us (5%)
  between operations  13.9 us (3%)
  starting transfers between devices  13.5 us (3%)
    add x9, local copies, waits for them, and re-layouts, per_offset(): forward_part[0] * backward_part[1] + forward_part[2] * backward_part[3]  168 us
    psum x1, waiting for transfers between devices, local(): summed = lax.psum(coarse, 'shot')  67.5 us
    reduce_sum x9, other arithmetic, coarsen(): image_block.reshape(size_x // 4, 4, size_y // 4, 4, size_z // 4, 4)  63.6 us
    another operation x1, loops' own time, offset_image(): return lax.map(per_offset, offsets)  22.5 us
    add x9, other arithmetic, per_offset(): forward_part[0] * backward_part[1] + forward_part[2] * backward_part[3]  15.1 us
    scatter-add x4, other arithmetic, inject(): jnp.zeros((cells_here * plane_size + 1,), jnp.float32).at[target]  11.9 us
    ppermute x2, starting transfers between devices, padded_2(): lax.ppermute(lax.slice_in_dim(block, block.shape[dim] - width, None, axis...  9.52 us
  transfers between devices with their start and end apart: 5, of which 4 were waited for; matrix products, arithmetic and copies ran while one was open for 3% of the time, Pallas kernels for 0%

commit v1 on v0

v1 whole, which is shorter than its diff:
```python
import functools

import jax
import jax.numpy as jnp
from jax import lax
from jax.experimental import pallas as pl
from jax.experimental.pallas import tpu as pltpu
from jax.sharding import PartitionSpec as P

HMAX = 8
MESH = pl.DeviceIdType.MESH


def kernel(
    dims,
    sp_ref,
    sn_ref,
    rp_ref,
    rn_ref,
    courant_ref,
    scells_ref,
    wavelet_ref,
    rcells_ref,
    rdata_ref,
    offsets_ref,
    weight_ref,
    out_ref,
    now,
    prev,
    cour,
    first_lev,
    second_lev,
    inj,
    acc,
    pads,
    padi,
    rows,
    parts,
    summed,
    patches,
    load_sem,
    edge_send,
    edge_recv,
    lev_send,
    lev_recv,
    row_send,
    row_recv,
    rim_send,
    rim_recv,
):
    shots, slabs, cells, size_y, size_z, count = dims
    me_shot = lax.axis_index("shot")
    me_gx = lax.axis_index("gx")
    has_left = me_gx > 0
    has_right = me_gx < slabs - 1
    left = {"gx": me_gx - 1}
    right = {"gx": me_gx + 1}
    coarse_x, coarse_y, coarse_z = cells // 4, size_y // 4, size_z // 4
    own_rows = coarse_y // shots
    window = own_rows + 2
    H = HMAX
    lev = (first_lev, second_lev)

    loads = [
        pltpu.make_async_copy(sn_ref.at[0], now.at[0, pl.ds(1, cells)], load_sem.at[0]),
        pltpu.make_async_copy(rn_ref.at[0], now.at[1, pl.ds(1, cells)], load_sem.at[1]),
        pltpu.make_async_copy(sp_ref.at[0], prev.at[0], load_sem.at[2]),
        pltpu.make_async_copy(rp_ref.at[0], prev.at[1], load_sem.at[3]),
        pltpu.make_async_copy(courant_ref, cour, load_sem.at[4]),
    ]
    for load in loads:
        load.start()

    barrier = pltpu.get_barrier_semaphore()
    for step in range(1, shots):
        pl.semaphore_signal(
            barrier,
            inc=1,
            device_id={"shot": lax.rem(me_shot + step, shots)},
            device_id_type=MESH,
        )

    @pl.when(has_left)
    def _():
        pl.semaphore_signal(barrier, inc=1, device_id=left, device_id_type=MESH)

    @pl.when(has_right)
    def _():
        pl.semaphore_signal(barrier, inc=1, device_id=right, device_id_type=MESH)

    pl.semaphore_wait(
        barrier, shots - 1 + has_left.astype(jnp.int32) + has_right.astype(jnp.int32)
    )

    def remote(src, dst, send, recv, target):
        return pltpu.make_async_remote_copy(
            src_ref=src,
            dst_ref=dst,
            send_sem=send,
            recv_sem=recv,
            device_id=target,
            device_id_type=MESH,
        )

    def edge_copy(field, side):
        source = (sn_ref, rn_ref)[field]
        plane, place = ((0, cells + 1), (cells - 1, 0))[side]
        return remote(
            source.at[0, pl.ds(plane, 1)],
            now.at[field, pl.ds(place, 1)],
            edge_send.at[field, side],
            edge_recv.at[field, side],
            (left, right)[side],
        )

    def level_copy(step, field, side, part):
        if side == 0:
            first, size = ((1, H - 1), (0, 1))[part]
            place = H + cells + first
        else:
            first, size = ((cells - H, H - 1), (cells - 1, 1))[part]
            place = first - cells + H
        return remote(
            lev[step].at[field, pl.ds(H + first, size)],
            lev[step].at[field, pl.ds(place, size)],
            lev_send.at[step, field, side, part],
            lev_recv.at[step, field, side, part],
            (left, right)[side],
        )

    def goes(side):
        return (has_left, has_right)[side]

    def comes(side):
        return (has_right, has_left)[side]

    def start(copy, side):
        @pl.when(goes(side))
        def _():
            copy.start()

    def wait_send(copy, side):
        @pl.when(goes(side))
        def _():
            copy.wait_send()

    def wait_recv(copy, side):
        @pl.when(comes(side))
        def _():
            copy.wait_recv()

    for field in range(2):
        for side in range(2):
            start(edge_copy(field, side), side)

    zero_plane = jnp.zeros((size_y, size_z), jnp.float32)

    @pl.when(jnp.logical_not(has_left))
    def _():
        for field in range(2):
            now[field, 0] = zero_plane
            for step in range(2):
                lev[step][field, 0:H] = jnp.zeros((H, size_y, size_z), jnp.float32)

    @pl.when(jnp.logical_not(has_right))
    def _():
        for field in range(2):
            now[field, cells + 1] = zero_plane
            for step in range(2):
                lev[step][field, H + cells : H + cells + H] = jnp.zeros(
                    (H, size_y, size_z), jnp.float32
                )

    z_bits = size_z.bit_length() - 1
    first_row = me_gx * (cells * size_y)

    def columns(cell, amps):
        lanes = cell.shape[-1]
        z_of = jnp.bitwise_and(cell, size_z - 1)
        hit = lax.broadcasted_iota(jnp.int32, (size_z, lanes), 0) == z_of
        pieces = []
        for amp in amps:
            high = amp.astype(jnp.bfloat16).astype(jnp.float32)
            for piece in (high, amp - high):
                pieces.append(jnp.where(hit, piece, 0.0).astype(jnp.bfloat16))
        return jnp.concatenate(pieces, axis=0)

    def spread(field, cell, amps):
        lanes = cell.shape[-1]
        right_side = columns(cell, amps)
        row_of = jnp.right_shift(cell, z_bits) - first_row
        block = 4 * size_y

        def body(step, carry):
            first = step * block
            row = lax.broadcasted_iota(jnp.int32, (block, lanes), 0) + first
            hit = jnp.where(row == row_of, 1.0, 0.0).astype(jnp.bfloat16)
            value = lax.dot_general(
                hit, right_side, (((1,), (1,)), ((), ())), preferred_element_type=jnp.float32
            )
            at = pl.ds(pl.multiple_of(first, block), block)
            inj[0, field, at] = value[:, 0:size_z] + value[:, size_z : 2 * size_z]
            inj[1, field, at] = value[:, 2 * size_z : 3 * size_z] + value[:, 3 * size_z :]
            return carry

        lax.fori_loop(0, cells * size_y // block, body, 0)

    few = scells_ref.shape[-1]
    padi[...] = jnp.full(padi.shape, -1, jnp.int32)
    pads[...] = jnp.zeros(pads.shape, jnp.float32)
    padi[0:1, 0:few] = scells_ref[...]
    pads[0:2, 0:few] = wavelet_ref[0]
    spread(0, padi[0:1], (pads[0:1], pads[1:2]))
    spread(1, rcells_ref[...], (rdata_ref[0, 0:1], rdata_ref[0, 1:2]))

    row_index = lax.broadcasted_iota(jnp.int32, (size_y, size_z), 0)
    lane_index = lax.broadcasted_iota(jnp.int32, (size_y, size_z), 1)

    def advance(before, low, center, high, speed, source):
        total = low + high
        total = total + jnp.where(row_index == 0, 0.0, pltpu.roll(center, 1, 0))
        total = total + jnp.where(row_index == size_y - 1, 0.0, pltpu.roll(center, size_y - 1, 0))
        total = total + jnp.where(lane_index == 0, 0.0, pltpu.roll(center, 1, 1))
        total = total + jnp.where(lane_index == size_z - 1, 0.0, pltpu.roll(center, size_z - 1, 1))
        return 2.0 * center - before + speed * (total - 6.0 * center) + source

    def first_level(x):
        speed = cour[x]
        for field in range(2):
            source = inj[0, field, pl.ds(pl.multiple_of(x * size_y, size_y), size_y)]
            lev[0][field, H + x] = advance(
                prev[field, x], now[field, x], now[field, x + 1], now[field, x + 2], speed, source
            )

    def second_level(x):
        speed = cour[x]
        for field in range(2):
            source = inj[1, field, pl.ds(pl.multiple_of(x * size_y, size_y), size_y)]
            lev[1][field, H + x] = advance(
                now[field, x + 1],
                lev[0][field, H + x - 1],
                lev[0][field, H + x],
                lev[0][field, H + x + 1],
                speed,
                source,
            )

    def planes(one, first, last):
        def body(x, carry):
            one(x)
            return carry

        lax.fori_loop(first, last, body, 0)

    def inner_planes(step, one):
        planes(one, cells - H, cells - 1)
        for field in range(2):
            start(level_copy(step, field, 1, 0), 1)
        planes(one, 1, cells - H)
        for field in range(2):
            start(level_copy(step, field, 0, 0), 0)

    def outer_planes(step, one):
        one(0)
        one(cells - 1)
        for field in range(2):
            for side in range(2):
                start(level_copy(step, field, side, 1), side)

    for load in loads:
        load.wait()
    inner_planes(0, first_level)
    for field in range(2):
        for side in range(2):
            wait_recv(edge_copy(field, side), side)
    outer_planes(0, first_level)
    inner_planes(1, second_level)
    for field in range(2):
        for side in range(2):
            wait_recv(level_copy(0, field, side, 1), side)
    outer_planes(1, second_level)

    def products(step):
        def body(item, carry):
            which = item // coarse_x
            block = item % coarse_x
            offset = offsets_ref[which]
            total = (
                lev[step][0, H + offset + block * 4] * lev[step][1, H - offset + block * 4]
            )
            for inner in range(1, 4):
                total = total + (
                    lev[step][0, H + offset + block * 4 + inner]
                    * lev[step][1, H - offset + block * 4 + inner]
                )
            if step == 0:
                acc[which, block] = total
            else:
                acc[which, block] = acc[which, block] + total
            return carry

        lax.fori_loop(0, count * coarse_x, body, 0)

    for field in range(2):
        for side in range(2):
            wait_recv(level_copy(0, field, side, 0), side)
    products(0)
    for field in range(2):
        for side in range(2):
            wait_recv(level_copy(1, field, side, 0), side)
            wait_recv(level_copy(1, field, side, 1), side)
    products(1)

    lanes = coarse_x * coarse_z
    deep = coarse_x * size_z
    z_row = lax.broadcasted_iota(jnp.int32, (deep, lanes), 0)
    z_col = lax.broadcasted_iota(jnp.int32, (deep, lanes), 1)
    mean = jnp.where(jnp.right_shift(z_row, 2) == z_col, 1.0 / 64.0, 0.0)
    wide = []
    for which in range(count):
        by_x = []
        for block in range(coarse_x):
            total = acc[which, block, pl.ds(0, coarse_y, stride=4)]
            for inner in range(1, 4):
                total = total + acc[which, block, pl.ds(inner, coarse_y, stride=4)]
            by_x.append(total)
        wide.append(jnp.concatenate(by_x, axis=1))
    coarse = jnp.dot(
        jnp.concatenate(wide, axis=0),
        mean,
        precision=lax.Precision.HIGHEST,
        preferred_element_type=jnp.float32,
    )
    rows[0] = jnp.zeros((count, lanes), jnp.float32)
    rows[coarse_y + 1] = jnp.zeros((count, lanes), jnp.float32)
    for which in range(count):
        for y in range(coarse_y):
            line = which * coarse_y + y
            rows[1 + y, which : which + 1] = coarse[line : line + 1]

    def row_copy(step):
        target = lax.rem(me_shot + step, shots)
        return remote(
            rows.at[pl.ds(target * own_rows, window)],
            parts.at[step],
            row_send.at[step],
            row_recv.at[step],
            {"shot": target},
        )

    for step in range(1, shots):
        row_copy(step).start()
    total = rows[pl.ds(me_shot * own_rows, window)]
    for step in range(1, shots):
        row_copy(step).wait_recv()
        total = total + parts[step]
    summed[1] = jnp.zeros(summed.shape[1:], jnp.float32)
    summed[1, :, 0:count] = total

    def rim_copy(side):
        return remote(
            summed.at[1],
            summed.at[(2, 0)[side]],
            rim_send.at[side],
            rim_recv.at[side],
            (left, right)[side],
        )

    for side in range(2):
        start(rim_copy(side), side)

    @pl.when(jnp.logical_not(has_left))
    def _():
        summed[0] = jnp.zeros(summed.shape[1:], jnp.float32)

    @pl.when(jnp.logical_not(has_right))
    def _():
        summed[2] = jnp.zeros(summed.shape[1:], jnp.float32)

    for side in range(2):
        wait_recv(rim_copy(side), side)

    flat = (window * 16, lanes)
    lane = lax.broadcasted_iota(jnp.int32, flat, 1)
    z_lane = jnp.bitwise_and(lane, coarse_z - 1)
    low, own, high = (summed[place].reshape(flat) for place in range(3))
    shifted = (
        jnp.where(lane < coarse_z, pltpu.roll(low, coarse_z, 1), pltpu.roll(own, coarse_z, 1)),
        own,
        jnp.where(
            lane >= lanes - coarse_z,
            pltpu.roll(high, lanes - coarse_z, 1),
            pltpu.roll(own, lanes - coarse_z, 1),
        ),
    )
    for a in range(3):
        patches[a * 3] = jnp.where(z_lane == 0, 0.0, pltpu.roll(shifted[a], 1, 1))
        patches[a * 3 + 1] = shifted[a]
        patches[a * 3 + 2] = jnp.where(
            z_lane == coarse_z - 1, 0.0, pltpu.roll(shifted[a], lanes - 1, 1)
        )
    for y in range(own_rows):
        tall = jnp.concatenate([patches[k, y * 16 : y * 16 + 48] for k in range(9)], axis=0)
        out_ref[:, y * lanes : (y + 1) * lanes] = jnp.dot(
            weight_ref[...],
            tall,
            precision=lax.Precision.HIGHEST,
            preferred_element_type=jnp.float32,
        )

    for field in range(2):
        for side in range(2):
            wait_send(edge_copy(field, side), side)
            for step in range(2):
                for part in range(2):
                    wait_send(level_copy(step, field, side, part), side)
    for step in range(1, shots):
        row_copy(step).wait_send()
    for side in range(2):
        wait_send(rim_copy(side), side)


def local(
    source_prev,
    source_now,
    receiver_prev,
    receiver_now,
    courant,
    source_cells,
    wavelet,
    receiver_cells,
    receiver_data,
    offsets,
    conv_weight,
    conv_bias,
):
    cells, size_y, size_z = courant.shape
    shots, slabs = lax.axis_size("shot"), lax.axis_size("gx")
    count = offsets.shape[0]
    channels = conv_weight.shape[0]
    coarse_x, coarse_y, coarse_z = cells // 4, size_y // 4, size_z // 4
    own_rows = coarse_y // shots
    window = own_rows + 2
    lanes = coarse_x * coarse_z
    weight = jnp.pad(
        conv_weight.transpose(0, 2, 4, 3, 1), ((0, 0), (0, 0), (0, 0), (0, 0), (0, 16 - count))
    ).reshape(channels, 27 * 16)

    anywhere = pl.BlockSpec(memory_space=pl.ANY)
    vmem = pl.BlockSpec(memory_space=pltpu.VMEM)
    smem = pl.BlockSpec(memory_space=pltpu.SMEM)
    f32 = jnp.float32
    result = pl.pallas_call(
        functools.partial(kernel, (shots, slabs, cells, size_y, size_z, count)),
        out_shape=jax.ShapeDtypeStruct((channels, own_rows * lanes), f32),
        in_specs=[anywhere] * 5 + [vmem] * 4 + [smem, vmem],
        out_specs=vmem,
        scratch_shapes=[
            pltpu.VMEM((2, cells + 2, size_y, size_z), f32),
            pltpu.VMEM((2, cells, size_y, size_z), f32),
            pltpu.VMEM((cells, size_y, size_z), f32),
            pltpu.VMEM((2, cells + 2 * HMAX, size_y, size_z), f32),
            pltpu.VMEM((2, cells + 2 * HMAX, size_y, size_z), f32),
            pltpu.VMEM((2, 2, cells * size_y, size_z), f32),
            pltpu.VMEM((count, coarse_x, size_y, size_z), f32),
            pltpu.VMEM((8, 128), f32),
            pltpu.VMEM((8, 128), jnp.int32),
            pltpu.VMEM((coarse_y + 2, count, lanes), f32),
            pltpu.VMEM((shots, window, count, lanes), f32),
            pltpu.VMEM((3, window, 16, lanes), f32),
            pltpu.VMEM((9, window * 16, lanes), f32),
            pltpu.SemaphoreType.DMA((5,)),
            pltpu.SemaphoreType.DMA((2, 2)),
            pltpu.SemaphoreType.DMA((2, 2)),
            pltpu.SemaphoreType.DMA((2, 2, 2, 2)),
            pltpu.SemaphoreType.DMA((2, 2, 2, 2)),
            pltpu.SemaphoreType.DMA((shots,)),
            pltpu.SemaphoreType.DMA((shots,)),
            pltpu.SemaphoreType.DMA((2,)),
            pltpu.SemaphoreType.DMA((2,)),
        ],
        compiler_params=pltpu.CompilerParams(
            collective_id=0, has_side_effects=True, vmem_limit_bytes=32 * 1024 * 1024
        ),
        cost_estimate=pl.CostEstimate(
            flops=1_500_000_000, bytes_accessed=3_000_000, transcendentals=0
        ),
    )(
        source_prev,
        source_now,
        receiver_prev,
        receiver_now,
        courant,
        source_cells,
        wavelet,
        receiver_cells,
        receiver_data,
        offsets,
        weight,
    )
    result = result.reshape(channels, own_rows, coarse_x, coarse_z).transpose(0, 2, 1, 3)
    return result.reshape(channels, coarse_x, own_rows * coarse_z) + conv_bias[:, None, None]


def solution(mesh):
    in_specs = (
        P("shot", "gx", None, None),
        P("shot", "gx", None, None),
        P("shot", "gx", None, None),
        P("shot", "gx", None, None),
        P("gx", None, None),
        P("shot", None),
        P("shot", None, None),
        P("shot", None),
        P("shot", None, None),
        P(),
        P(),
        P(),
    )
    out_specs = P(None, "gx", "shot")
    return jax.shard_map(local, mesh=mesh, in_specs=in_specs, out_specs=out_specs, check_vma=False)
```

time: 427 us -> 38.4 us (0.09)
  the two profiles are of different devices: /device:TPU:25 before, /device:TPU:1 now
where the time goes in v1:
time: 38.4 us; the launch traced here: 38.1 us
  Pallas kernels  31.6 us (82%)
  local copies, waits for them, and re-layouts  6.37 us (17%)
    pallas_call x1, Pallas kernels, local(): pl.pallas_call(functools.partial(kernel, (shots, slabs, cells, size_y, si...  31.6 us
    unnamed x23, local copies, waits for them, and re-layouts  5.39 us

profile of v1, /device:TPU:1, one launch (start us, length us, event | category | flops | bytes accessed | tf_op | source)
XLA Modules:
  0.0 38.1 jit_solution(16670606613566531830)
XLA Ops:
  0.0 0.0 copy-start
  0.0 0.0 copy-start.1
  0.0 1.0 %copy.20 = f32[64,3,3,3,9]{0,4,3,2,1:T(8,128)S(1)} copy(f32[64,3,3,3,9]{0,2,3,1,4:T(4,128)} %bitcast.9) | data formatting | bytes 124416
  1.1 0.0 copy-start.5
  1.1 0.0 copy-start.6
  1.1 0.0 copy-start.7
  1.1 0.0 copy-start.8
  1.1 0.0 copy-start.9
  1.1 0.1 copy.16.weight_ref
  1.2 0.0 copy-done
  1.3 0.0 copy-done.1
  1.3 0.5 %copy-done.5 = f32[1,2,512]{2,1,0:T(2,128)S(1)} copy-done((f32[1,2,512]{2,1,0:T(2,128)S(1)}, f32[1,2,512]{2,1,0:T(2,128)}, u32[]{:S(2)}) %copy-start.5) | copy-done | bytes 4120
  1.8 0.0 copy-done.6
  1.8 0.0 copy-done.7
  1.8 0.0 copy-done.8
  1.8 0.0 copy-done.9
  1.8 1.0 %copy-done.2 = f32[1,16,64,128]{3,2,1,0:T(8,128)S(1)} copy-done((f32[1,16,64,128]{3,2,1,0:T(8,128)S(1)}, f32[1,16,64,128]{3,2,1,0:T(8,128)}, u32[]{:S(2)}) %copy-start.2) | copy-done | bytes 524312
  2.9 1.0 %copy-done.3 = f32[1,16,64,128]{3,2,1,0:T(8,128)S(1)} copy-done((f32[1,16,64,128]{3,2,1,0:T(8,128)S(1)}, f32[1,16,64,128]{3,2,1,0:T(8,128)}, u32[]{:S(2)}) %copy-start.3) | copy-done | bytes 524312
  3.9 1.0 %copy-done.4 = f32[16,64,128]{2,1,0:T(8,128)S(1)} copy-done((f32[16,64,128]{2,1,0:T(8,128)S(1)}, f32[16,64,128]{2,1,0:T(8,128)}, u32[]{:S(2)}) %copy-start.4) | copy-done | bytes 524312
  5.0 31.6 %shard_map.118 = f32[64,256]{1,0:T(8,128)S(1)} custom-call(f32[1,16,64,128]{3,2,1,0:T(8,128)S(1)} %copy-done, f32[1,16,64,128]{3,2,1,0:T(8,128)S(1)} %copy-done.1, f32[1,16,64,128]{3,2,1,0:T(8,128)S(1)} %copy-done.2, f32[1,16,64,128]{3,2,1,0:T(8,128)S(1)} %copy-done.3, f32[16,64,128]{2,1,0:T(8,128)S(1)} %copy-done.4, s32[1,8]{1,0:T(1,128)S(1)} %copy-done.8, ...), custom_call_target="tpu_custom_call" | custom-call | flops 1500000000 | bytes 3000000 | tf_op jit(solution)/shard_map/pallas_call | solution.py:453
  36.6 0.1 copy.17
  36.7 0.0 copy-start.10
  36.7 0.6 %copy-done.10 = f32[64]{0:T(128)S(1)} copy-done((f32[64]{0:T(128)S(1)}, f32[64]{0:T(128)}, u32[]{:S(2)}) %copy-start.10) | copy-done | bytes 280
  37.4 0.8 %copy.19 = f32[64,4,64]{2,1,0:T(4,128)} copy(f32[64,4,64]{0,2,1:T(8,128)S(1)} %bitcast_add_fusion) | data formatting | bytes 131072 | tf_op jit(solution)/shard_map/add | solution.py:502
  (6 shorter events, 0.0 us)
Async XLA Ops:
  0.0 1.2 %copy-start = (f32[1,16,64,128]{3,2,1,0:T(8,128)S(1)}, f32[1,16,64,128]{3,2,1,0:T(8,128)}, u32[]{:S(2)}) copy-start(f32[1,16,64,128]{3,2,1,0:T(8,128)} %sp_ref.1) | copy-start | bytes 1572868
  0.0 1.3 %copy-start.1 = (f32[1,16,64,128]{3,2,1,0:T(8,128)S(1)}, f32[1,16,64,128]{3,2,1,0:T(8,128)}, u32[]{:S(2)}) copy-start(f32[1,16,64,128]{3,2,1,0:T(8,128)} %sn_ref.1) | copy-start | bytes 1572868
  1.1 0.7 %copy-start.5 = (f32[1,2,512]{2,1,0:T(2,128)S(1)}, f32[1,2,512]{2,1,0:T(2,128)}, u32[]{:S(2)}) copy-start(f32[1,2,512]{2,1,0:T(2,128)} %rdata_ref.1) | copy-start | bytes 12292
  1.1 0.7 %copy-start.6 = (s32[1,512]{1,0:T(1,128)S(1)}, s32[1,512]{1,0:T(1,128)}, u32[]{:S(2)}) copy-start(s32[1,512]{1,0:T(1,128)} %rcells_ref.1) | copy-start | bytes 6148
  1.1 0.7 %copy-start.7 = (f32[1,2,8]{2,1,0:T(2,128)S(1)}, f32[1,2,8]{2,1,0:T(2,128)}, u32[]{:S(2)}) copy-start(f32[1,2,8]{2,1,0:T(2,128)} %wavelet_ref.1) | copy-start | bytes 196
  1.1 0.7 %copy-start.8 = (s32[1,8]{1,0:T(1,128)S(1)}, s32[1,8]{1,0:T(1,128)}, u32[]{:S(2)}) copy-start(s32[1,8]{1,0:T(1,128)} %scells_ref.1) | copy-start | bytes 100
  1.1 0.7 %copy-start.9 = (s32[9]{0:T(128)S(1)}, s32[9]{0:T(128)}, u32[]{:S(2)}) copy-start(s32[9]{0:T(128)} %offsets_ref.1) | copy-start | bytes 112
  1.8 1.0 %copy-start.2 = (f32[1,16,64,128]{3,2,1,0:T(8,128)S(1)}, f32[1,16,64,128]{3,2,1,0:T(8,128)}, u32[]{:S(2)}) copy-start(f32[1,16,64,128]{3,2,1,0:T(8,128)} %rp_ref.1) | copy-start | bytes 1572868
  2.9 1.0 %copy-start.3 = (f32[1,16,64,128]{3,2,1,0:T(8,128)S(1)}, f32[1,16,64,128]{3,2,1,0:T(8,128)}, u32[]{:S(2)}) copy-start(f32[1,16,64,128]{3,2,1,0:T(8,128)} %rn_ref.1) | copy-start | bytes 1572868
  3.9 1.0 %copy-start.4 = (f32[16,64,128]{2,1,0:T(8,128)S(1)}, f32[16,64,128]{2,1,0:T(8,128)}, u32[]{:S(2)}) copy-start(f32[16,64,128]{2,1,0:T(8,128)} %courant_ref.1) | copy-start | bytes 1572868
  36.7 0.7 %copy-start.10 = (f32[64]{0:T(128)S(1)}, f32[64]{0:T(128)}, u32[]{:S(2)}) copy-start(f32[64]{0:T(128)} %param.23) | copy-start | bytes 772

commit v2 on v1

v2 whole, which is shorter than its diff:
```python
import functools

import jax
import jax.numpy as jnp
from jax import lax
from jax.experimental import pallas as pl
from jax.experimental.pallas import tpu as pltpu
from jax.sharding import PartitionSpec as P

HMAX = 8
HALVES = 2
MESH = pl.DeviceIdType.MESH


def kernel(
    dims,
    sp_ref,
    sn_ref,
    rp_ref,
    rn_ref,
    courant_ref,
    scells_ref,
    wavelet_ref,
    rcells_ref,
    rdata_ref,
    offsets_ref,
    weight_ref,
    bias_ref,
    out_ref,
    now,
    prev,
    cour,
    first_lev,
    second_low,
    second_high,
    inj,
    acc,
    pads,
    padi,
    rows,
    parts,
    summed,
    patches,
    conv_in,
    tall,
    load_sem,
    edge_send,
    edge_recv,
    lev_send,
    lev_recv,
    row_send,
    row_recv,
    rim_send,
    rim_recv,
    late_send,
    late_recv,
):
    shots, slabs, cells, size_y, size_z, count = dims
    me_shot = lax.axis_index("shot")
    me_gx = lax.axis_index("gx")
    has_left = me_gx > 0
    has_right = me_gx < slabs - 1
    left = {"gx": me_gx - 1}
    right = {"gx": me_gx + 1}
    coarse_x, coarse_y, coarse_z = cells // 4, size_y // 4, size_z // 4
    own_rows = coarse_y // shots
    window = own_rows + 2
    H = HMAX
    second = (second_low, second_high)
    half_y = size_y // HALVES
    half_rows = coarse_y // HALVES

    loads = [
        pltpu.make_async_copy(sn_ref.at[0], now.at[0, pl.ds(1, cells)], load_sem.at[0]),
        pltpu.make_async_copy(rn_ref.at[0], now.at[1, pl.ds(1, cells)], load_sem.at[1]),
        pltpu.make_async_copy(sp_ref.at[0], prev.at[0], load_sem.at[2]),
        pltpu.make_async_copy(rp_ref.at[0], prev.at[1], load_sem.at[3]),
        pltpu.make_async_copy(courant_ref, cour, load_sem.at[4]),
    ]
    for load in loads:
        load.start()
    weight_load = pltpu.make_async_copy(weight_ref, conv_in, load_sem.at[5])
    weight_load.start()

    barrier = pltpu.get_barrier_semaphore()
    for step in range(1, shots):
        pl.semaphore_signal(
            barrier,
            inc=1,
            device_id={"shot": lax.rem(me_shot + step, shots)},
            device_id_type=MESH,
        )

    @pl.when(has_left)
    def _():
        pl.semaphore_signal(barrier, inc=1, device_id=left, device_id_type=MESH)

    @pl.when(has_right)
    def _():
        pl.semaphore_signal(barrier, inc=1, device_id=right, device_id_type=MESH)

    def remote(src, dst, send, recv, target):
        return pltpu.make_async_remote_copy(
            src_ref=src,
            dst_ref=dst,
            send_sem=send,
            recv_sem=recv,
            device_id=target,
            device_id_type=MESH,
        )

    def edge_copy(field, side):
        source = (sn_ref, rn_ref)[field]
        plane, place = ((0, cells + 1), (cells - 1, 0))[side]
        return remote(
            source.at[0, pl.ds(plane, 1)],
            now.at[field, pl.ds(place, 1)],
            edge_send.at[field, side],
            edge_recv.at[field, side],
            (left, right)[side],
        )

    def place_of(side, part):
        if side == 0:
            first, size = ((1, H - 1), (0, 1))[part]
            return first, size, H + cells + first
        first, size = ((cells - H, H - 1), (cells - 1, 1))[part]
        return first, size, first - cells + H

    def first_copy(field, side, part):
        first, size, place = place_of(side, part)
        return remote(
            first_lev.at[field, pl.ds(H + first, size)],
            first_lev.at[field, pl.ds(place, size)],
            lev_send.at[field, side, part],
            lev_recv.at[field, side, part],
            (left, right)[side],
        )

    def second_copy(half, field, side, part):
        first, size, place = place_of(side, part)
        return remote(
            second[half].at[field, pl.ds(H + first, size)],
            second[half].at[field, pl.ds(place, size)],
            late_send.at[half, field, side, part],
            late_recv.at[half, field, side, part],
            (left, right)[side],
        )

    both = [(field, side) for field in range(2) for side in range(2)]

    def goes(side):
        return (has_left, has_right)[side]

    def comes(side):
        return (has_right, has_left)[side]

    def start(copy, side):
        @pl.when(goes(side))
        def _():
            copy.start()

    def wait_send(copy, side):
        @pl.when(goes(side))
        def _():
            copy.wait_send()

    def wait_recv(copy, side):
        @pl.when(comes(side))
        def _():
            copy.wait_recv()

    zero_plane = jnp.zeros((size_y, size_z), jnp.float32)

    def clear(plane, place):
        for field in range(2):
            now[field, plane] = zero_plane
            first_lev[field, place : place + H] = jnp.zeros((H, size_y, size_z), jnp.float32)
            for half in range(HALVES):
                second[half][field, place : place + H] = jnp.zeros(
                    (H, half_y, size_z), jnp.float32
                )

    @pl.when(jnp.logical_not(has_left))
    def _():
        clear(0, 0)

    @pl.when(jnp.logical_not(has_right))
    def _():
        clear(cells + 1, H + cells)

    z_bits = size_z.bit_length() - 1
    first_row = me_gx * (cells * size_y)

    def spread(step, field, cell, amp):
        lanes = cell.shape[-1]
        z_of = jnp.bitwise_and(cell, size_z - 1)
        there = lax.broadcasted_iota(jnp.int32, (size_z, lanes), 0) == z_of
        high = amp.astype(jnp.bfloat16).astype(jnp.float32)
        pieces = [
            jnp.where(there, piece, 0.0).astype(jnp.bfloat16) for piece in (high, amp - high)
        ]
        right_side = jnp.concatenate(pieces, axis=0)
        row_of = jnp.right_shift(cell, z_bits) - first_row
        block = 4 * size_y

        def body(item, carry):
            first = item * block
            row = lax.broadcasted_iota(jnp.int32, (block, lanes), 0) + first
            hit = jnp.where(row == row_of, 1.0, 0.0).astype(jnp.bfloat16)
            value = lax.dot_general(
                hit, right_side, (((1,), (1,)), ((), ())), preferred_element_type=jnp.float32
            )
            at = pl.ds(pl.multiple_of(first, block), block)
            inj[step, field, at] = value[:, 0:size_z] + value[:, size_z:]
            return carry

        lax.fori_loop(0, cells * size_y // block, body, 0)

    few = scells_ref.shape[-1]
    padi[...] = jnp.full(padi.shape, -1, jnp.int32)
    pads[...] = jnp.zeros(pads.shape, jnp.float32)
    padi[0:1, 0:few] = scells_ref[...]
    pads[0:2, 0:few] = wavelet_ref[0]

    def injection(step):
        spread(step, 0, padi[0:1], pads[step : step + 1])
        spread(step, 1, rcells_ref[...], rdata_ref[0, step : step + 1])

    injection(0)

    pl.semaphore_wait(
        barrier, shots - 1 + has_left.astype(jnp.int32) + has_right.astype(jnp.int32)
    )

    for field, side in both:
        start(edge_copy(field, side), side)

    row_index = lax.broadcasted_iota(jnp.int32, (size_y, size_z), 0)
    lane_index = lax.broadcasted_iota(jnp.int32, (size_y, size_z), 1)

    def advance(before, low, center, high, speed, source):
        total = low + high
        total = total + jnp.where(row_index == 0, 0.0, pltpu.roll(center, 1, 0))
        total = total + jnp.where(row_index == size_y - 1, 0.0, pltpu.roll(center, size_y - 1, 0))
        total = total + jnp.where(lane_index == 0, 0.0, pltpu.roll(center, 1, 1))
        total = total + jnp.where(lane_index == size_z - 1, 0.0, pltpu.roll(center, size_z - 1, 1))
        return 2.0 * center - before + speed * (total - 6.0 * center) + source

    def first_level(x):
        speed = cour[x]
        for field in range(2):
            source = inj[0, field, pl.ds(pl.multiple_of(x * size_y, size_y), size_y)]
            first_lev[field, H + x] = advance(
                prev[field, x], now[field, x], now[field, x + 1], now[field, x + 2], speed, source
            )

    def second_level(x):
        speed = cour[x]
        for field in range(2):
            source = inj[1, field, pl.ds(pl.multiple_of(x * size_y, size_y), size_y)]
            value = advance(
                now[field, x + 1],
                first_lev[field, H + x - 1],
                first_lev[field, H + x],
                first_lev[field, H + x + 1],
                speed,
                source,
            )
            for half in range(HALVES):
                second[half][field, H + x] = value[half * half_y : (half + 1) * half_y]

    def planes(one, first, last):
        def body(x, carry):
            one(x)
            return carry

        lax.fori_loop(first, last, body, 0, unroll=True)

    for load in loads:
        load.wait()
    planes(first_level, cells - H, cells - 1)
    for field in range(2):
        start(first_copy(field, 1, 0), 1)
    planes(first_level, 1, cells - H)
    for field in range(2):
        start(first_copy(field, 0, 0), 0)
    for field, side in both:
        wait_recv(edge_copy(field, side), side)
    first_level(0)
    first_level(cells - 1)
    for field, side in both:
        start(first_copy(field, side, 1), side)

    injection(1)
    planes(second_level, cells - H, cells - 1)
    for field in range(2):
        start(second_copy(0, field, 1, 0), 1)
    planes(second_level, 1, cells - H)
    for field in range(2):
        start(second_copy(0, field, 0, 0), 0)
    for field, side in both:
        wait_recv(first_copy(field, side, 1), side)
    second_level(0)
    second_level(cells - 1)
    for half in range(HALVES):
        for field, side in both:
            start(second_copy(half, field, side, 1), side)
    for field, side in both:
        start(second_copy(1, field, side, 0), side)

    weight_load.wait()
    tall[...] = jnp.zeros(tall.shape, jnp.float32)
    for which in range(count):
        for a in range(3):
            for b in range(3):
                for c in range(3):
                    line = ((a * 3 + c) * 3 + b) * 16 + which
                    tall[line : line + 1] = conv_in[which, a, b, c : c + 1]
    line = 13 * 16 + count
    tall[line : line + 1] = bias_ref[...]
    matrix = tall[...].T

    def products(level, rows_here, first):
        def body(which, carry):
            offset = offsets_ref[which]
            for block in range(coarse_x):
                total = None
                for inner in range(4):
                    x = H + block * 4 + inner
                    term = level[0, x + offset] * level[1, x - offset]
                    total = term if total is None else total + term
                if first:
                    acc[which, block] = total
                else:
                    acc[which, block, rows_here] = acc[which, block, rows_here] + total
            return carry

        lax.fori_loop(0, count, body, 0)

    lanes = coarse_x * coarse_z
    deep = coarse_x * size_z
    z_row = lax.broadcasted_iota(jnp.int32, (deep, lanes), 0)
    z_col = lax.broadcasted_iota(jnp.int32, (deep, lanes), 1)
    mean = jnp.where(jnp.right_shift(z_row, 2) == z_col, 1.0 / 64.0, 0.0)
    rows[0] = jnp.zeros((count, lanes), jnp.float32)
    rows[coarse_y + 1] = jnp.zeros((count, lanes), jnp.float32)

    def means(half):
        wide = []
        for which in range(count):
            by_x = []
            for block in range(coarse_x):
                total = None
                for inner in range(4):
                    term = acc[which, block, pl.ds(half * half_y + inner, half_rows, stride=4)]
                    total = term if total is None else total + term
                by_x.append(total)
            wide.append(jnp.concatenate(by_x, axis=1))
        coarse = jnp.dot(
            jnp.concatenate(wide, axis=0),
            mean,
            precision=lax.Precision.HIGHEST,
            preferred_element_type=jnp.float32,
        )
        for which in range(count):
            for y in range(half_rows):
                line = which * half_rows + y
                rows[1 + half * half_rows + y, which : which + 1] = coarse[line : line + 1]

    def row_copy(source, target):
        return remote(
            rows.at[pl.ds(target * own_rows, window)],
            parts.at[source],
            row_send.at[target],
            row_recv.at[source],
            {"shot": target},
        )

    def send_rows(targets):
        for target in targets:

            @pl.when(me_shot != target)
            def _():
                row_copy(me_shot, target).start()

    for field, side in both:
        wait_recv(first_copy(field, side, 0), side)
    products(first_lev, slice(0, size_y), True)
    sent = 0
    for half in range(HALVES):
        for field, side in both:
            wait_recv(second_copy(half, field, side, 1), side)
            wait_recv(second_copy(half, field, side, 0), side)
        products(second[half], slice(half * half_y, (half + 1) * half_y), False)
        means(half)
        done = shots if half == HALVES - 1 else ((half + 1) * half_rows + 1 - window) // own_rows + 1
        send_rows(range(sent, done))
        sent = done
    parts[me_shot] = rows[pl.ds(me_shot * own_rows, window)]
    total = None
    for source in range(shots):

        @pl.when(me_shot != source)
        def _():
            row_copy(source, source).wait_recv()

        total = parts[source] if total is None else total + parts[source]
    summed[1] = jnp.zeros(summed.shape[1:], jnp.float32)
    summed[1, :, 0:count] = total
    summed[1, :, count : count + 1] = jnp.ones((window, 1, lanes), jnp.float32)

    def rim_copy(side):
        return remote(
            summed.at[1],
            summed.at[(2, 0)[side]],
            rim_send.at[side],
            rim_recv.at[side],
            (left, right)[side],
        )

    for side in range(2):
        start(rim_copy(side), side)

    @pl.when(jnp.logical_not(has_left))
    def _():
        summed[0] = jnp.zeros(summed.shape[1:], jnp.float32)

    @pl.when(jnp.logical_not(has_right))
    def _():
        summed[2] = jnp.zeros(summed.shape[1:], jnp.float32)

    for side in range(2):
        wait_recv(rim_copy(side), side)

    flat = (window * 16, lanes)
    lane = lax.broadcasted_iota(jnp.int32, flat, 1)
    z_lane = jnp.bitwise_and(lane, coarse_z - 1)
    low, own, high = (summed[place].reshape(flat) for place in range(3))
    shifted = (
        jnp.where(lane < coarse_z, pltpu.roll(low, coarse_z, 1), pltpu.roll(own, coarse_z, 1)),
        own,
        jnp.where(
            lane >= lanes - coarse_z,
            pltpu.roll(high, lanes - coarse_z, 1),
            pltpu.roll(own, lanes - coarse_z, 1),
        ),
    )
    for a in range(3):
        patches[a * 3] = jnp.where(z_lane == 0, 0.0, pltpu.roll(shifted[a], 1, 1))
        patches[a * 3 + 1] = shifted[a]
        patches[a * 3 + 2] = jnp.where(
            z_lane == coarse_z - 1, 0.0, pltpu.roll(shifted[a], lanes - 1, 1)
        )
    for y in range(own_rows):
        deep_rows = jnp.concatenate([patches[k, y * 16 : y * 16 + 48] for k in range(9)], axis=0)
        out_ref[:, y * lanes : (y + 1) * lanes] = jnp.dot(
            matrix,
            deep_rows,
            precision=lax.Precision.HIGHEST,
            preferred_element_type=jnp.float32,
        )

    for field, side in both:
        wait_send(edge_copy(field, side), side)
        for part in range(2):
            wait_send(first_copy(field, side, part), side)
            for half in range(HALVES):
                wait_send(second_copy(half, field, side, part), side)
    for target in range(shots):

        @pl.when(me_shot != target)
        def _():
            row_copy(me_shot, target).wait_send()

    for side in range(2):
        wait_send(rim_copy(side), side)


def local(
    source_prev,
    source_now,
    receiver_prev,
    receiver_now,
    courant,
    source_cells,
    wavelet,
    receiver_cells,
    receiver_data,
    offsets,
    conv_weight,
    conv_bias,
):
    cells, size_y, size_z = courant.shape
    shots, slabs = lax.axis_size("shot"), lax.axis_size("gx")
    count = offsets.shape[0]
    channels = conv_weight.shape[0]
    coarse_x, coarse_y, coarse_z = cells // 4, size_y // 4, size_z // 4
    own_rows = coarse_y // shots
    window = own_rows + 2
    lanes = coarse_x * coarse_z
    anywhere = pl.BlockSpec(memory_space=pltpu.HBM)
    vmem = pl.BlockSpec(memory_space=pltpu.VMEM)
    smem = pl.BlockSpec(memory_space=pltpu.SMEM)
    f32 = jnp.float32
    result = pl.pallas_call(
        functools.partial(kernel, (shots, slabs, cells, size_y, size_z, count)),
        out_shape=jax.ShapeDtypeStruct((channels, own_rows * lanes), f32),
        in_specs=[anywhere] * 5 + [vmem] * 4 + [smem, anywhere, vmem],
        out_specs=vmem,
        scratch_shapes=[
            pltpu.VMEM((2, cells + 2, size_y, size_z), f32),
            pltpu.VMEM((2, cells, size_y, size_z), f32),
            pltpu.VMEM((cells, size_y, size_z), f32),
            pltpu.VMEM((2, cells + 2 * HMAX, size_y, size_z), f32),
            pltpu.VMEM((2, cells + 2 * HMAX, size_y // HALVES, size_z), f32),
            pltpu.VMEM((2, cells + 2 * HMAX, size_y // HALVES, size_z), f32),
            pltpu.VMEM((2, 2, cells * size_y, size_z), f32),
            pltpu.VMEM((count, coarse_x, size_y, size_z), f32),
            pltpu.VMEM((8, 128), f32),
            pltpu.VMEM((8, 128), jnp.int32),
            pltpu.VMEM((coarse_y + 2, count, lanes), f32),
            pltpu.VMEM((shots, window, count, lanes), f32),
            pltpu.VMEM((3, window, 16, lanes), f32),
            pltpu.VMEM((9, window * 16, lanes), f32),
            pltpu.VMEM((count, 3, 3, 3, channels), f32),
            pltpu.VMEM((27 * 16, channels), f32),
            pltpu.SemaphoreType.DMA((6,)),
            pltpu.SemaphoreType.DMA((2, 2)),
            pltpu.SemaphoreType.DMA((2, 2)),
            pltpu.SemaphoreType.DMA((2, 2, 2)),
            pltpu.SemaphoreType.DMA((2, 2, 2)),
            pltpu.SemaphoreType.DMA((shots,)),
            pltpu.SemaphoreType.DMA((shots,)),
            pltpu.SemaphoreType.DMA((2,)),
            pltpu.SemaphoreType.DMA((2,)),
            pltpu.SemaphoreType.DMA((HALVES, 2, 2, 2)),
            pltpu.SemaphoreType.DMA((HALVES, 2, 2, 2)),
        ],
        compiler_params=pltpu.CompilerParams(
            collective_id=0, has_side_effects=True, vmem_limit_bytes=64 * 1024 * 1024 - 256 * 1024
        ),
        cost_estimate=pl.CostEstimate(
            flops=1_500_000_000, bytes_accessed=3_000_000, transcendentals=0
        ),
    )(
        source_prev,
        source_now,
        receiver_prev,
        receiver_now,
        courant,
        source_cells,
        wavelet,
        receiver_cells,
        receiver_data,
        offsets,
        conv_weight.transpose(1, 2, 3, 4, 0),
        conv_bias.reshape(1, channels),
    )
    result = result.reshape(channels, own_rows, coarse_x, coarse_z).transpose(0, 2, 1, 3)
    return result.reshape(channels, coarse_x, own_rows * coarse_z)


def solution(mesh):
    in_specs = (
        P("shot", "gx", None, None),
        P("shot", "gx", None, None),
        P("shot", "gx", None, None),
        P("shot", "gx", None, None),
        P("gx", None, None),
        P("shot", None),
        P("shot", None, None),
        P("shot", None),
        P("shot", None, None),
        P(),
        P(),
        P(),
    )
    out_specs = P(None, "gx", "shot")
    return jax.shard_map(local, mesh=mesh, in_specs=in_specs, out_specs=out_specs, check_vma=False)
```

time: 38.4 us -> 30 us (0.78)
  the two profiles are of different devices: /device:TPU:1 before, /device:TPU:25 now
where the time goes in v2:
time: 30 us; the launch traced here: 29.7 us
  Pallas kernels  28 us (93%)
  local copies, waits for them, and re-layouts  1.7 us (6%)
    pallas_call x1, Pallas kernels, local(): pl.pallas_call(functools.partial(kernel, (shots, slabs, cells, size_y, si...  28 us
    pallas_call x1, local copies, waits for them, and re-layouts, local(): pl.pallas_call(functools.partial(kernel, (shots, slabs, cells, size_y, si...  0.93 us
    reshape x1, local copies, waits for them, and re-layouts, local(): return result.reshape(channels, coarse_x, own_rows * coarse_z)  0.76 us

profile of v2, /device:TPU:25, one launch (start us, length us, event | category | flops | bytes accessed | tf_op | source)
XLA Modules:
  0.0 29.7 jit_solution(4006998741310473739)
XLA Ops:
  0.0 28.0 %shard_map.118 = f32[64,256]{1,0:T(8,128)} custom-call(f32[1,16,64,128]{3,2,1,0:T(8,128)} %sp_ref.1, f32[1,16,64,128]{3,2,1,0:T(8,128)} %sn_ref.1, f32[1,16,64,128]{3,2,1,0:T(8,128)} %rp_ref.1, f32[1,16,64,128]{3,2,1,0:T(8,128)} %rn_ref.1, f32[16,64,128]{2,1,0:T(8,128)} %courant_ref.1, s32[1,8]{1,0:T(1,128)} %scells_ref.1, f32[1,2,8]{2,1,0:T(2,128)} %wavelet_ref.1, ...), custom_call_target="tpu_custom_call" | custom-call | flops 1500000000 | bytes 3000000 | tf_op jit(solution)/shard_map/pallas_call | solution.py:506
  28.0 0.9 %copy.14 = f32[64,256]{0,1:T(8,128)S(1)} copy(f32[64,256]{1,0:T(8,128)} %shard_map.118) | data formatting | bytes 131072 | tf_op jit(solution)/shard_map/pallas_call | solution.py:506
  28.9 0.8 %copy.16 = f32[64,4,64]{2,1,0:T(4,128)} copy(f32[64,4,64]{0,2,1:T(8,128)S(1)} %bitcast.7) | data formatting | bytes 131072 | tf_op jit(solution)/shard_map/reshape | solution.py:561
  (1 shorter events, 0.0 us)

commit v3 on v2

--- a/solution.py
+++ b/solution.py
@@ -202,7 +202,7 @@
         ]
         right_side = jnp.concatenate(pieces, axis=0)
         row_of = jnp.right_shift(cell, z_bits) - first_row
-        block = 4 * size_y
+        block = 8 * size_y
 
         def body(item, carry):
             first = item * block
@@ -215,7 +215,7 @@
             inj[step, field, at] = value[:, 0:size_z] + value[:, size_z:]
             return carry
 
-        lax.fori_loop(0, cells * size_y // block, body, 0)
+        lax.fori_loop(0, cells * size_y // block, body, 0, unroll=True)
 
     few = scells_ref.shape[-1]
     padi[...] = jnp.full(padi.shape, -1, jnp.int32)
@@ -309,6 +309,16 @@
     for field, side in both:
         start(second_copy(1, field, side, 0), side)
 
+    def split(value, pieces):
+        out = []
+        for _ in range(pieces):
+            out.append(value.astype(jnp.bfloat16))
+            value = value - out[-1].astype(jnp.float32)
+        return out
+
+    def dot(one, other):
+        return jnp.dot(one, other, preferred_element_type=jnp.float32)
+
     weight_load.wait()
     tall[...] = jnp.zeros(tall.shape, jnp.float32)
     for which in range(count):
@@ -318,8 +328,11 @@
                     line = ((a * 3 + c) * 3 + b) * 16 + which
                     tall[line : line + 1] = conv_in[which, a, b, c : c + 1]
     line = 13 * 16 + count
-    tall[line : line + 1] = bias_ref[...]
-    matrix = tall[...].T
+    bias = bias_ref[...]
+    tall[line : line + 1] = bias.astype(jnp.bfloat16).astype(jnp.float32)
+    tall[line + 1 : line + 2] = bias - bias.astype(jnp.bfloat16).astype(jnp.float32)
+    matrix_high, matrix_low = split(tall[...].T, 2)
+    matrix_both = jnp.concatenate([matrix_high, matrix_low], axis=0)
 
     def products(level, rows_here, first):
         def body(which, carry):
@@ -342,7 +355,7 @@
     deep = coarse_x * size_z
     z_row = lax.broadcasted_iota(jnp.int32, (deep, lanes), 0)
     z_col = lax.broadcasted_iota(jnp.int32, (deep, lanes), 1)
-    mean = jnp.where(jnp.right_shift(z_row, 2) == z_col, 1.0 / 64.0, 0.0)
+    mean = jnp.where(jnp.right_shift(z_row, 2) == z_col, 1.0 / 64.0, 0.0).astype(jnp.bfloat16)
     rows[0] = jnp.zeros((count, lanes), jnp.float32)
     rows[coarse_y + 1] = jnp.zeros((count, lanes), jnp.float32)
 
@@ -357,12 +370,9 @@
                     total = term if total is None else total + term
                 by_x.append(total)
             wide.append(jnp.concatenate(by_x, axis=1))
-        coarse = jnp.dot(
-            jnp.concatenate(wide, axis=0),
-            mean,
-            precision=lax.Precision.HIGHEST,
-            preferred_element_type=jnp.float32,
-        )
+        high = count * half_rows
+        product = dot(jnp.concatenate(split(jnp.concatenate(wide, axis=0), 3), axis=0), mean)
+        coarse = product[:high] + product[high : 2 * high] + product[2 * high :]
         for which in range(count):
             for y in range(half_rows):
                 line = which * half_rows + y
@@ -408,7 +418,7 @@
         total = parts[source] if total is None else total + parts[source]
     summed[1] = jnp.zeros(summed.shape[1:], jnp.float32)
     summed[1, :, 0:count] = total
-    summed[1, :, count : count + 1] = jnp.ones((window, 1, lanes), jnp.float32)
+    summed[1, :, count : count + 2] = jnp.ones((window, 2, lanes), jnp.float32)
 
     def rim_copy(side):
         return remote(
@@ -452,14 +462,20 @@
         patches[a * 3 + 2] = jnp.where(
             z_lane == coarse_z - 1, 0.0, pltpu.roll(shifted[a], lanes - 1, 1)
         )
-    for y in range(own_rows):
-        deep_rows = jnp.concatenate([patches[k, y * 16 : y * 16 + 48] for k in range(9)], axis=0)
-        out_ref[:, y * lanes : (y + 1) * lanes] = jnp.dot(
-            matrix,
-            deep_rows,
-            precision=lax.Precision.HIGHEST,
-            preferred_element_type=jnp.float32,
-        )
+    columns = [
+        jnp.concatenate([patches[k, y * 16 : y * 16 + 48] for k in range(9)], axis=0)
+        for y in range(own_rows)
+    ]
+    columns_high, columns_low = split(jnp.concatenate(columns, axis=1), 2)
+    channels = matrix_high.shape[0]
+    product = dot(matrix_both, columns_high)
+    product = product[:channels] + product[channels:] + dot(matrix_high, columns_low)
+    for x in range(coarse_x):
+        pieces = [
+            product[:, y * lanes + x * coarse_z : y * lanes + (x + 1) * coarse_z]
+            for y in range(own_rows)
+        ]
+        out_ref[pl.ds(x, channels, stride=coarse_x)] = jnp.concatenate(pieces, axis=1)
 
     for field, side in both:
         wait_send(edge_copy(field, side), side)
@@ -505,7 +521,7 @@
     f32 = jnp.float32
     result = pl.pallas_call(
         functools.partial(kernel, (shots, slabs, cells, size_y, size_z, count)),
-        out_shape=jax.ShapeDtypeStruct((channels, own_rows * lanes), f32),
+        out_shape=jax.ShapeDtypeStruct((channels * coarse_x, own_rows * coarse_z), f32),
         in_specs=[anywhere] * 5 + [vmem] * 4 + [smem, anywhere, vmem],
         out_specs=vmem,
         scratch_shapes=[
@@ -557,7 +573,6 @@
         conv_weight.transpose(1, 2, 3, 4, 0),
         conv_bias.reshape(1, channels),
     )
-    result = result.reshape(channels, own_rows, coarse_x, coarse_z).transpose(0, 2, 1, 3)
     return result.reshape(channels, coarse_x, own_rows * coarse_z)
 
 

time: 30 us -> 29.7 us (0.990)
    unnamed x0 -> x1, local copies, waits for them, and re-layouts: none -> 1.57 us
    pallas_call x1 -> x0, local copies, waits for them, and re-layouts: 0.93 us -> none  [local(): pl.pallas_call(functools.partial(kernel, (shots, slabs, cells, size_y, si...]
    reshape x1 -> x0, local copies, waits for them, and re-layouts: 0.76 us -> none  [local(): return result.reshape(channels, coarse_x, own_rows * coarse_z)]
where the time goes in v3:
time: 29.7 us; the launch traced here: 29.4 us
  Pallas kernels  27.9 us (94%)
  local copies, waits for them, and re-layouts  1.57 us (5%)
    pallas_call x1, Pallas kernels, local(): pl.pallas_call(functools.partial(kernel, (shots, slabs, cells, size_y, si...  27.9 us
    unnamed x1, local copies, waits for them, and re-layouts  1.57 us

profile of v3, /device:TPU:25, one launch (start us, length us, event | category | flops | bytes accessed | tf_op | source)
XLA Modules:
  0.0 29.4 jit_solution(4486241755344521215)
XLA Ops:
  0.0 27.9 %shard_map.118 = f32[256,64]{1,0:T(8,128)} custom-call(f32[1,16,64,128]{3,2,1,0:T(8,128)} %sp_ref.1, f32[1,16,64,128]{3,2,1,0:T(8,128)} %sn_ref.1, f32[1,16,64,128]{3,2,1,0:T(8,128)} %rp_ref.1, f32[1,16,64,128]{3,2,1,0:T(8,128)} %rn_ref.1, f32[16,64,128]{2,1,0:T(8,128)} %courant_ref.1, s32[1,8]{1,0:T(1,128)} %scells_ref.1, f32[1,2,8]{2,1,0:T(2,128)} %wavelet_ref.1, ...), custom_call_target="tpu_custom_call" | custom-call | flops 1500000000 | bytes 3000000 | tf_op jit(solution)/shard_map/pallas_call | solution.py:522
  27.9 1.6 %copy.14 = f32[64,4,64]{2,1,0:T(4,128)} copy(f32[64,4,64]{2,1,0:T(4,128)} %bitcast.3) | data formatting | bytes 131072

commit v4 on v3

--- a/solution.py
+++ b/solution.py
@@ -9,6 +9,7 @@
 
 HMAX = 8
 HALVES = 2
+RIM = 2
 MESH = pl.DeviceIdType.MESH
 
 
@@ -71,11 +72,11 @@
     half_rows = coarse_y // HALVES
 
     loads = [
-        pltpu.make_async_copy(sn_ref.at[0], now.at[0, pl.ds(1, cells)], load_sem.at[0]),
-        pltpu.make_async_copy(rn_ref.at[0], now.at[1, pl.ds(1, cells)], load_sem.at[1]),
+        pltpu.make_async_copy(sn_ref.at[0], now.at[0, pl.ds(RIM, cells)], load_sem.at[0]),
+        pltpu.make_async_copy(rn_ref.at[0], now.at[1, pl.ds(RIM, cells)], load_sem.at[1]),
         pltpu.make_async_copy(sp_ref.at[0], prev.at[0], load_sem.at[2]),
         pltpu.make_async_copy(rp_ref.at[0], prev.at[1], load_sem.at[3]),
-        pltpu.make_async_copy(courant_ref, cour, load_sem.at[4]),
+        pltpu.make_async_copy(courant_ref, cour.at[pl.ds(RIM, cells)], load_sem.at[4]),
     ]
     for load in loads:
         load.start()
@@ -98,6 +99,10 @@
     @pl.when(has_right)
     def _():
         pl.semaphore_signal(barrier, inc=1, device_id=right, device_id_type=MESH)
+
+    pl.semaphore_wait(
+        barrier, shots - 1 + has_left.astype(jnp.int32) + has_right.astype(jnp.int32)
+    )
 
     def remote(src, dst, send, recv, target):
         return pltpu.make_async_remote_copy(
@@ -109,14 +114,15 @@
             device_id_type=MESH,
         )
 
-    def edge_copy(field, side):
-        source = (sn_ref, rn_ref)[field]
-        plane, place = ((0, cells + 1), (cells - 1, 0))[side]
+    def edge_copy(kind, side):
+        source = (sn_ref.at[0], rn_ref.at[0], courant_ref)[kind]
+        target = (now.at[0], now.at[1], cour)[kind]
+        plane, place = ((0, cells + RIM), (cells - RIM, 0))[side]
         return remote(
-            source.at[0, pl.ds(plane, 1)],
-            now.at[field, pl.ds(place, 1)],
-            edge_send.at[field, side],
-            edge_recv.at[field, side],
+            source.at[pl.ds(plane, RIM)],
+            target.at[pl.ds(place, RIM)],
+            edge_send.at[kind, side],
+            edge_recv.at[kind, side],
             (left, right)[side],
         )
 
@@ -137,17 +143,19 @@
             (left, right)[side],
         )
 
-    def second_copy(half, field, side, part):
-        first, size, place = place_of(side, part)
+    def second_copy(half, field, side):
+        size = H - RIM
+        first, place = ((RIM, H + cells + RIM), (cells - H, 0))[side]
         return remote(
             second[half].at[field, pl.ds(H + first, size)],
             second[half].at[field, pl.ds(place, size)],
-            late_send.at[half, field, side, part],
-            late_recv.at[half, field, side, part],
+            late_send.at[half, field, side],
+            late_recv.at[half, field, side],
             (left, right)[side],
         )
 
     both = [(field, side) for field in range(2) for side in range(2)]
+    edges = [(kind, side) for kind in range(3) for side in range(2)]
 
     def goes(side):
         return (has_left, has_right)[side]
@@ -170,11 +178,12 @@
         def _():
             copy.wait_recv()
 
-    zero_plane = jnp.zeros((size_y, size_z), jnp.float32)
+    for kind, side in edges:
+        start(edge_copy(kind, side), side)
 
     def clear(plane, place):
         for field in range(2):
-            now[field, plane] = zero_plane
+            now[field, plane : plane + RIM] = jnp.zeros((RIM, size_y, size_z), jnp.float32)
             first_lev[field, place : place + H] = jnp.zeros((H, size_y, size_z), jnp.float32)
             for half in range(HALVES):
                 second[half][field, place : place + H] = jnp.zeros(
@@ -187,7 +196,7 @@
 
     @pl.when(jnp.logical_not(has_right))
     def _():
-        clear(cells + 1, H + cells)
+        clear(cells + RIM, H + cells)
 
     z_bits = size_z.bit_length() - 1
     first_row = me_gx * (cells * size_y)
@@ -201,8 +210,10 @@
             jnp.where(there, piece, 0.0).astype(jnp.bfloat16) for piece in (high, amp - high)
         ]
         right_side = jnp.concatenate(pieces, axis=0)
-        row_of = jnp.right_shift(cell, z_bits) - first_row
-        block = 8 * size_y
+        extra = 0 if step == 0 else RIM
+        count_x = cells + 2 * extra
+        row_of = jnp.right_shift(cell, z_bits) - first_row + extra * size_y
+        block = (8 if count_x % 8 == 0 else 4) * size_y
 
         def body(item, carry):
             first = item * block
@@ -215,7 +226,7 @@
             inj[step, field, at] = value[:, 0:size_z] + value[:, size_z:]
             return carry
 
-        lax.fori_loop(0, cells * size_y // block, body, 0, unroll=True)
+        lax.fori_loop(0, count_x * size_y // block, body, 0, unroll=True)
 
     few = scells_ref.shape[-1]
     padi[...] = jnp.full(padi.shape, -1, jnp.int32)
@@ -228,13 +239,6 @@
         spread(step, 1, rcells_ref[...], rdata_ref[0, step : step + 1])
 
     injection(0)
-
-    pl.semaphore_wait(
-        barrier, shots - 1 + has_left.astype(jnp.int32) + has_right.astype(jnp.int32)
-    )
-
-    for field, side in both:
-        start(edge_copy(field, side), side)
 
     row_index = lax.broadcasted_iota(jnp.int32, (size_y, size_z), 0)
     lane_index = lax.broadcasted_iota(jnp.int32, (size_y, size_z), 1)
@@ -248,19 +252,25 @@
         return 2.0 * center - before + speed * (total - 6.0 * center) + source
 
     def first_level(x):
-        speed = cour[x]
+        speed = cour[RIM + x]
         for field in range(2):
             source = inj[0, field, pl.ds(pl.multiple_of(x * size_y, size_y), size_y)]
             first_lev[field, H + x] = advance(
-                prev[field, x], now[field, x], now[field, x + 1], now[field, x + 2], speed, source
+                prev[field, x],
+                now[field, RIM + x - 1],
+                now[field, RIM + x],
+                now[field, RIM + x + 1],
+                speed,
+                source,
             )
 
     def second_level(x):
-        speed = cour[x]
+        speed = cour[RIM + x]
         for field in range(2):
-            source = inj[1, field, pl.ds(pl.multiple_of(x * size_y, size_y), size_y)]
+            line = pl.multiple_of((RIM + x) * size_y, size_y)
+            source = inj[1, field, pl.ds(line, size_y)]
             value = advance(
-                now[field, x + 1],
+                now[field, RIM + x],
                 first_lev[field, H + x - 1],
                 first_lev[field, H + x],
                 first_lev[field, H + x + 1],
@@ -293,21 +303,29 @@
         start(first_copy(field, side, 1), side)
 
     injection(1)
-    planes(second_level, cells - H, cells - 1)
-    for field in range(2):
-        start(second_copy(0, field, 1, 0), 1)
-    planes(second_level, 1, cells - H)
-    for field in range(2):
-        start(second_copy(0, field, 0, 0), 0)
+    planes(second_level, cells - H, cells - RIM)
+    for half in range(HALVES):
+        for field in range(2):
+            start(second_copy(half, field, 1), 1)
+    planes(second_level, RIM, cells - H)
+    for half in range(HALVES):
+        for field in range(2):
+            start(second_copy(half, field, 0), 0)
     for field, side in both:
         wait_recv(first_copy(field, side, 1), side)
-    second_level(0)
-    second_level(cells - 1)
-    for half in range(HALVES):
-        for field, side in both:
-            start(second_copy(half, field, side, 1), side)
-    for field, side in both:
-        start(second_copy(1, field, side, 0), side)
+        wait_recv(first_copy(field, side, 0), side)
+    for side in range(2):
+        wait_recv(edge_copy(2, side), side)
+    planes(second_level, 0, RIM)
+    planes(second_level, cells - RIM, cells)
+
+    @pl.when(has_left)
+    def _():
+        planes(second_level, -RIM, 0)
+
+    @pl.when(has_right)
+    def _():
+        planes(second_level, cells, cells + RIM)
 
     def split(value, pieces):
         out = []
@@ -394,14 +412,11 @@
             def _():
                 row_copy(me_shot, target).start()
 
-    for field, side in both:
-        wait_recv(first_copy(field, side, 0), side)
     products(first_lev, slice(0, size_y), True)
     sent = 0
     for half in range(HALVES):
         for field, side in both:
-            wait_recv(second_copy(half, field, side, 1), side)
-            wait_recv(second_copy(half, field, side, 0), side)
+            wait_recv(second_copy(half, field, side), side)
         products(second[half], slice(half * half_y, (half + 1) * half_y), False)
         means(half)
         done = shots if half == HALVES - 1 else ((half + 1) * half_rows + 1 - window) // own_rows + 1
@@ -477,12 +492,13 @@
         ]
         out_ref[pl.ds(x, channels, stride=coarse_x)] = jnp.concatenate(pieces, axis=1)
 
+    for kind, side in edges:
+        wait_send(edge_copy(kind, side), side)
     for field, side in both:
-        wait_send(edge_copy(field, side), side)
         for part in range(2):
             wait_send(first_copy(field, side, part), side)
-            for half in range(HALVES):
-                wait_send(second_copy(half, field, side, part), side)
+        for half in range(HALVES):
+            wait_send(second_copy(half, field, side), side)
     for target in range(shots):
 
         @pl.when(me_shot != target)
@@ -521,17 +537,17 @@
     f32 = jnp.float32
     result = pl.pallas_call(
         functools.partial(kernel, (shots, slabs, cells, size_y, size_z, count)),
-        out_shape=jax.ShapeDtypeStruct((channels * coarse_x, own_rows * coarse_z), f32),
+        out_shape=pltpu.VMEM((channels * coarse_x, own_rows * coarse_z), f32),
         in_specs=[anywhere] * 5 + [vmem] * 4 + [smem, anywhere, vmem],
         out_specs=vmem,
         scratch_shapes=[
-            pltpu.VMEM((2, cells + 2, size_y, size_z), f32),
+            pltpu.VMEM((2, cells + 2 * RIM, size_y, size_z), f32),
             pltpu.VMEM((2, cells, size_y, size_z), f32),
-            pltpu.VMEM((cells, size_y, size_z), f32),
+            pltpu.VMEM((cells + 2 * RIM, size_y, size_z), f32),
             pltpu.VMEM((2, cells + 2 * HMAX, size_y, size_z), f32),
             pltpu.VMEM((2, cells + 2 * HMAX, size_y // HALVES, size_z), f32),
             pltpu.VMEM((2, cells + 2 * HMAX, size_y // HALVES, size_z), f32),
-            pltpu.VMEM((2, 2, cells * size_y, size_z), f32),
+            pltpu.VMEM((2, 2, (cells + 2 * RIM) * size_y, size_z), f32),
             pltpu.VMEM((count, coarse_x, size_y, size_z), f32),
             pltpu.VMEM((8, 128), f32),
             pltpu.VMEM((8, 128), jnp.int32),
@@ -542,19 +558,19 @@
             pltpu.VMEM((count, 3, 3, 3, channels), f32),
             pltpu.VMEM((27 * 16, channels), f32),
             pltpu.SemaphoreType.DMA((6,)),
-            pltpu.SemaphoreType.DMA((2, 2)),
-            pltpu.SemaphoreType.DMA((2, 2)),
+            pltpu.SemaphoreType.DMA((3, 2)),
+            pltpu.SemaphoreType.DMA((3, 2)),
             pltpu.SemaphoreType.DMA((2, 2, 2)),
             pltpu.SemaphoreType.DMA((2, 2, 2)),
             pltpu.SemaphoreType.DMA((shots,)),
             pltpu.SemaphoreType.DMA((shots,)),
             pltpu.SemaphoreType.DMA((2,)),
             pltpu.SemaphoreType.DMA((2,)),
-            pltpu.SemaphoreType.DMA((HALVES, 2, 2, 2)),
-            pltpu.SemaphoreType.DMA((HALVES, 2, 2, 2)),
+            pltpu.SemaphoreType.DMA((HALVES, 2, 2)),
+            pltpu.SemaphoreType.DMA((HALVES, 2, 2)),
         ],
         compiler_params=pltpu.CompilerParams(
-            collective_id=0, has_side_effects=True, vmem_limit_bytes=64 * 1024 * 1024 - 256 * 1024
+            collective_id=0, has_side_effects=True, vmem_limit_bytes=63 * 1024 * 1024
         ),
         cost_estimate=pl.CostEstimate(
             flops=1_500_000_000, bytes_accessed=3_000_000, transcendentals=0

time: 29.7 us -> 27.1 us (0.912)
  Pallas kernels: 27.9 us -> 26.1 us
  local copies, waits for them, and re-layouts: 1.57 us -> 0.66 us
    pallas_call x1, Pallas kernels: 27.9 us -> 26.1 us  [local(): pl.pallas_call(functools.partial(kernel, (shots, slabs, cells, size_y, si...]
    unnamed x1, local copies, waits for them, and re-layouts: 1.57 us -> 0.66 us
where the time goes in v4:
time: 27.1 us; the launch traced here: 26.8 us
  Pallas kernels  26.1 us (96%)
  local copies, waits for them, and re-layouts  0.66 us (2%)
    pallas_call x1, Pallas kernels, local(): pl.pallas_call(functools.partial(kernel, (shots, slabs, cells, size_y, si...  26.1 us
    unnamed x1, local copies, waits for them, and re-layouts  0.66 us

profile of v4, /device:TPU:25, one launch (start us, length us, event | category | flops | bytes accessed | tf_op | source)
XLA Modules:
  0.0 26.8 jit_solution(10648009456010141401)
XLA Ops:
  0.0 26.1 %shard_map.118 = f32[256,64]{1,0:T(8,128)S(1)} custom-call(f32[1,16,64,128]{3,2,1,0:T(8,128)} %sp_ref.1, f32[1,16,64,128]{3,2,1,0:T(8,128)} %sn_ref.1, f32[1,16,64,128]{3,2,1,0:T(8,128)} %rp_ref.1, f32[1,16,64,128]{3,2,1,0:T(8,128)} %rn_ref.1, f32[16,64,128]{2,1,0:T(8,128)} %courant_ref.1, s32[1,8]{1,0:T(1,128)} %scells_ref.1, f32[1,2,8]{2,1,0:T(2,128)} %wavelet_ref.1, ...), custom_call_target="tpu_custom_call" | custom-call | flops 1500000000 | bytes 3000000 | tf_op jit(solution)/shard_map/pallas_call | solution.py:538
  26.1 0.7 %copy.14 = f32[64,4,64]{2,1,0:T(4,128)} copy(f32[64,4,64]{2,1,0:T(4,128)S(1)} %bitcast.3) | data formatting | bytes 131072

commit v5 on v4

--- a/solution.py
+++ b/solution.py
@@ -8,7 +8,7 @@
 from jax.sharding import PartitionSpec as P
 
 HMAX = 8
-HALVES = 2
+PARTS = 4
 RIM = 2
 MESH = pl.DeviceIdType.MESH
 
@@ -32,14 +32,17 @@
     prev,
     cour,
     first_lev,
-    second_low,
-    second_high,
+    second_0,
+    second_1,
+    second_2,
+    second_3,
     inj,
     acc,
     pads,
     padi,
     rows,
     parts,
+    rim,
     summed,
     patches,
     conv_in,
@@ -67,9 +70,9 @@
     own_rows = coarse_y // shots
     window = own_rows + 2
     H = HMAX
-    second = (second_low, second_high)
-    half_y = size_y // HALVES
-    half_rows = coarse_y // HALVES
+    second = (second_0, second_1, second_2, second_3)
+    half_y = size_y // PARTS
+    half_rows = coarse_y // PARTS
 
     loads = [
         pltpu.make_async_copy(sn_ref.at[0], now.at[0, pl.ds(RIM, cells)], load_sem.at[0]),
@@ -100,9 +103,32 @@
     def _():
         pl.semaphore_signal(barrier, inc=1, device_id=right, device_id_type=MESH)
 
-    pl.semaphore_wait(
-        barrier, shots - 1 + has_left.astype(jnp.int32) + has_right.astype(jnp.int32)
-    )
+    has_up = me_shot > 0
+    has_down = me_shot < shots - 1
+    beside = [(dy, dx) for dy in (-1, 0, 1) for dx in (-1, 0, 1) if (dy, dx) != (0, 0)]
+
+    def is_there(dy, dx):
+        there_y = (has_up, None, has_down)[1 + dy]
+        there_x = (has_left, None, has_right)[1 + dx]
+        if there_y is None:
+            return there_x
+        return there_y if there_x is None else jnp.logical_and(there_y, there_x)
+
+    def device_at(dy, dx):
+        return {"shot": me_shot + dy, "gx": me_gx + dx}
+
+    expected = shots - 1 + has_left.astype(jnp.int32) + has_right.astype(jnp.int32)
+    for dy in (-1, 1):
+        for dx in (-1, 1):
+            expected = expected + is_there(dy, dx).astype(jnp.int32)
+
+            @pl.when(is_there(dy, dx))
+            def _():
+                pl.semaphore_signal(
+                    barrier, inc=1, device_id=device_at(dy, dx), device_id_type=MESH
+                )
+
+    pl.semaphore_wait(barrier, expected)
 
     def remote(src, dst, send, recv, target):
         return pltpu.make_async_remote_copy(
@@ -185,7 +211,7 @@
         for field in range(2):
             now[field, plane : plane + RIM] = jnp.zeros((RIM, size_y, size_z), jnp.float32)
             first_lev[field, place : place + H] = jnp.zeros((H, size_y, size_z), jnp.float32)
-            for half in range(HALVES):
+            for half in range(PARTS):
                 second[half][field, place : place + H] = jnp.zeros(
                     (H, half_y, size_z), jnp.float32
                 )
@@ -277,7 +303,7 @@
                 speed,
                 source,
             )
-            for half in range(HALVES):
+            for half in range(PARTS):
                 second[half][field, H + x] = value[half * half_y : (half + 1) * half_y]
 
     def planes(one, first, last):
@@ -304,11 +330,11 @@
 
     injection(1)
     planes(second_level, cells - H, cells - RIM)
-    for half in range(HALVES):
+    for half in range(PARTS):
         for field in range(2):
             start(second_copy(half, field, 1), 1)
     planes(second_level, RIM, cells - H)
-    for half in range(HALVES):
+    for half in range(PARTS):
         for field in range(2):
             start(second_copy(half, field, 0), 0)
     for field, side in both:
@@ -374,8 +400,14 @@
     z_row = lax.broadcasted_iota(jnp.int32, (deep, lanes), 0)
     z_col = lax.broadcasted_iota(jnp.int32, (deep, lanes), 1)
     mean = jnp.where(jnp.right_shift(z_row, 2) == z_col, 1.0 / 64.0, 0.0).astype(jnp.bfloat16)
-    rows[0] = jnp.zeros((count, lanes), jnp.float32)
-    rows[coarse_y + 1] = jnp.zeros((count, lanes), jnp.float32)
+    summed[...] = jnp.zeros(summed.shape, jnp.float32)
+    summed[1, :, count : count + 2] = jnp.ones((window, 2, lanes), jnp.float32)
+    for dy, dx in beside:
+
+        @pl.when(jnp.logical_not(is_there(dy, dx)))
+        def _():
+            rim[1 + dy, 1 + dx] = jnp.zeros(rim.shape[2:], jnp.float32)
+
 
     def means(half):
         wide = []
@@ -394,11 +426,13 @@
         for which in range(count):
             for y in range(half_rows):
                 line = which * half_rows + y
-                rows[1 + half * half_rows + y, which : which + 1] = coarse[line : line + 1]
+                target, row = divmod(half * half_rows + y, own_rows)
+                at = row * count + which
+                rows[target, at : at + 1] = coarse[line : line + 1]
 
     def row_copy(source, target):
         return remote(
-            rows.at[pl.ds(target * own_rows, window)],
+            rows.at[target],
             parts.at[source],
             row_send.at[target],
             row_recv.at[source],
@@ -414,15 +448,15 @@
 
     products(first_lev, slice(0, size_y), True)
     sent = 0
-    for half in range(HALVES):
+    for half in range(PARTS):
         for field, side in both:
             wait_recv(second_copy(half, field, side), side)
         products(second[half], slice(half * half_y, (half + 1) * half_y), False)
         means(half)
-        done = shots if half == HALVES - 1 else ((half + 1) * half_rows + 1 - window) // own_rows + 1
+        done = (half + 1) * half_rows // own_rows
         send_rows(range(sent, done))
         sent = done
-    parts[me_shot] = rows[pl.ds(me_shot * own_rows, window)]
+    parts[me_shot] = rows[me_shot]
     total = None
     for source in range(shots):
 
@@ -431,32 +465,34 @@
             row_copy(source, source).wait_recv()
 
         total = parts[source] if total is None else total + parts[source]
-    summed[1] = jnp.zeros(summed.shape[1:], jnp.float32)
-    summed[1, :, 0:count] = total
-    summed[1, :, count : count + 2] = jnp.ones((window, 2, lanes), jnp.float32)
-
-    def rim_copy(side):
+    rim[1, 1] = total
+
+    def rim_copy(dy, dx):
         return remote(
-            summed.at[1],
-            summed.at[(2, 0)[side]],
-            rim_send.at[side],
-            rim_recv.at[side],
-            (left, right)[side],
-        )
-
-    for side in range(2):
-        start(rim_copy(side), side)
-
-    @pl.when(jnp.logical_not(has_left))
-    def _():
-        summed[0] = jnp.zeros(summed.shape[1:], jnp.float32)
-
-    @pl.when(jnp.logical_not(has_right))
-    def _():
-        summed[2] = jnp.zeros(summed.shape[1:], jnp.float32)
-
-    for side in range(2):
-        wait_recv(rim_copy(side), side)
+            rim.at[1, 1],
+            rim.at[1 - dy, 1 - dx],
+            rim_send.at[1 + dy, 1 + dx],
+            rim_recv.at[1 - dy, 1 - dx],
+            device_at(dy, dx),
+        )
+
+    for dy, dx in beside:
+
+        @pl.when(is_there(dy, dx))
+        def _():
+            rim_copy(dy, dx).start()
+
+    for dy, dx in beside:
+
+        @pl.when(is_there(dy, dx))
+        def _():
+            rim_copy(-dy, -dx).wait_recv()
+
+    for dx in range(3):
+        summed[dx, 0, 0:count] = rim[0, dx, (own_rows - 1) * count : own_rows * count]
+        for y in range(own_rows):
+            summed[dx, 1 + y, 0:count] = rim[1, dx, y * count : (y + 1) * count]
+        summed[dx, own_rows + 1, 0:count] = rim[2, dx, 0:count]
 
     flat = (window * 16, lanes)
     lane = lax.broadcasted_iota(jnp.int32, flat, 1)
@@ -497,7 +533,7 @@
     for field, side in both:
         for part in range(2):
             wait_send(first_copy(field, side, part), side)
-        for half in range(HALVES):
+        for half in range(PARTS):
             wait_send(second_copy(half, field, side), side)
     for target in range(shots):
 
@@ -505,8 +541,11 @@
         def _():
             row_copy(me_shot, target).wait_send()
 
-    for side in range(2):
-        wait_send(rim_copy(side), side)
+    for dy, dx in beside:
+
+        @pl.when(is_there(dy, dx))
+        def _():
+            rim_copy(dy, dx).wait_send()
 
 
 def local(
@@ -545,14 +584,17 @@
             pltpu.VMEM((2, cells, size_y, size_z), f32),
             pltpu.VMEM((cells + 2 * RIM, size_y, size_z), f32),
             pltpu.VMEM((2, cells + 2 * HMAX, size_y, size_z), f32),
-            pltpu.VMEM((2, cells + 2 * HMAX, size_y // HALVES, size_z), f32),
-            pltpu.VMEM((2, cells + 2 * HMAX, size_y // HALVES, size_z), f32),
+            pltpu.VMEM((2, cells + 2 * HMAX, size_y // PARTS, size_z), f32),
+            pltpu.VMEM((2, cells + 2 * HMAX, size_y // PARTS, size_z), f32),
+            pltpu.VMEM((2, cells + 2 * HMAX, size_y // PARTS, size_z), f32),
+            pltpu.VMEM((2, cells + 2 * HMAX, size_y // PARTS, size_z), f32),
             pltpu.VMEM((2, 2, (cells + 2 * RIM) * size_y, size_z), f32),
             pltpu.VMEM((count, coarse_x, size_y, size_z), f32),
             pltpu.VMEM((8, 128), f32),
             pltpu.VMEM((8, 128), jnp.int32),
-            pltpu.VMEM((coarse_y + 2, count, lanes), f32),
-            pltpu.VMEM((shots, window, count, lanes), f32),
+            pltpu.VMEM((shots, own_rows * count, lanes), f32),
+            pltpu.VMEM((shots, own_rows * count, lanes), f32),
+            pltpu.VMEM((3, 3, own_rows * count, lanes), f32),
             pltpu.VMEM((3, window, 16, lanes), f32),
             pltpu.VMEM((9, window * 16, lanes), f32),
             pltpu.VMEM((count, 3, 3, 3, channels), f32),
@@ -564,10 +606,10 @@
             pltpu.SemaphoreType.DMA((2, 2, 2)),
             pltpu.SemaphoreType.DMA((shots,)),
             pltpu.SemaphoreType.DMA((shots,)),
-            pltpu.SemaphoreType.DMA((2,)),
-            pltpu.SemaphoreType.DMA((2,)),
-            pltpu.SemaphoreType.DMA((HALVES, 2, 2)),
-            pltpu.SemaphoreType.DMA((HALVES, 2, 2)),
+            pltpu.SemaphoreType.DMA((3, 3)),
+            pltpu.SemaphoreType.DMA((3, 3)),
+            pltpu.SemaphoreType.DMA((PARTS, 2, 2)),
+            pltpu.SemaphoreType.DMA((PARTS, 2, 2)),
         ],
         compiler_params=pltpu.CompilerParams(
             collective_id=0, has_side_effects=True, vmem_limit_bytes=63 * 1024 * 1024

time: 27.1 us -> 27.2 us (level)
  no operation moved by 1% of the time
where the time goes in v5:
time: 27.2 us; the launch traced here: 27 us
  Pallas kernels  26.3 us (97%)
  local copies, waits for them, and re-layouts  0.66 us (2%)
    pallas_call x1, Pallas kernels, local(): pl.pallas_call(functools.partial(kernel, (shots, slabs, cells, size_y, si...  26.3 us
    unnamed x1, local copies, waits for them, and re-layouts  0.66 us

profile of v5, /device:TPU:25, one launch (start us, length us, event | category | flops | bytes accessed | tf_op | source)
XLA Modules:
  0.0 27.0 jit_solution(16055678390493173575)
XLA Ops:
  0.0 26.3 %shard_map.118 = f32[256,64]{1,0:T(8,128)S(1)} custom-call(f32[1,16,64,128]{3,2,1,0:T(8,128)} %sp_ref.1, f32[1,16,64,128]{3,2,1,0:T(8,128)} %sn_ref.1, f32[1,16,64,128]{3,2,1,0:T(8,128)} %rp_ref.1, f32[1,16,64,128]{3,2,1,0:T(8,128)} %rn_ref.1, f32[16,64,128]{2,1,0:T(8,128)} %courant_ref.1, s32[1,8]{1,0:T(1,128)} %scells_ref.1, f32[1,2,8]{2,1,0:T(2,128)} %wavelet_ref.1, ...), custom_call_target="tpu_custom_call" | custom-call | flops 1500000000 | bytes 3000000 | tf_op jit(solution)/shard_map/pallas_call | solution.py:577
  26.4 0.7 %copy.14 = f32[64,4,64]{2,1,0:T(4,128)} copy(f32[64,4,64]{2,1,0:T(4,128)S(1)} %bitcast.3) | data formatting | bytes 131072

commit v6 on v4

--- a/solution.py
+++ b/solution.py
@@ -133,24 +133,24 @@
         first, size = ((cells - H, H - 1), (cells - 1, 1))[part]
         return first, size, first - cells + H
 
-    def first_copy(field, side, part):
+    def first_copy(side, part):
         first, size, place = place_of(side, part)
         return remote(
-            first_lev.at[field, pl.ds(H + first, size)],
-            first_lev.at[field, pl.ds(place, size)],
-            lev_send.at[field, side, part],
-            lev_recv.at[field, side, part],
+            first_lev.at[:, pl.ds(H + first, size)],
+            first_lev.at[:, pl.ds(place, size)],
+            lev_send.at[side, part],
+            lev_recv.at[side, part],
             (left, right)[side],
         )
 
-    def second_copy(half, field, side):
+    def second_copy(half, side):
         size = H - RIM
         first, place = ((RIM, H + cells + RIM), (cells - H, 0))[side]
         return remote(
-            second[half].at[field, pl.ds(H + first, size)],
-            second[half].at[field, pl.ds(place, size)],
-            late_send.at[half, field, side],
-            late_recv.at[half, field, side],
+            second[half].at[:, pl.ds(H + first, size)],
+            second[half].at[:, pl.ds(place, size)],
+            late_send.at[half, side],
+            late_recv.at[half, side],
             (left, right)[side],
         )
 
@@ -290,43 +290,23 @@
     for load in loads:
         load.wait()
     planes(first_level, cells - H, cells - 1)
-    for field in range(2):
-        start(first_copy(field, 1, 0), 1)
+    start(first_copy(1, 0), 1)
     planes(first_level, 1, cells - H)
-    for field in range(2):
-        start(first_copy(field, 0, 0), 0)
+    start(first_copy(0, 0), 0)
     for field, side in both:
         wait_recv(edge_copy(field, side), side)
     first_level(0)
     first_level(cells - 1)
-    for field, side in both:
-        start(first_copy(field, side, 1), side)
+    for side in range(2):
+        start(first_copy(side, 1), side)
 
     injection(1)
     planes(second_level, cells - H, cells - RIM)
     for half in range(HALVES):
-        for field in range(2):
-            start(second_copy(half, field, 1), 1)
+        start(second_copy(half, 1), 1)
     planes(second_level, RIM, cells - H)
     for half in range(HALVES):
-        for field in range(2):
-            start(second_copy(half, field, 0), 0)
-    for field, side in both:
-        wait_recv(first_copy(field, side, 1), side)
-        wait_recv(first_copy(field, side, 0), side)
-    for side in range(2):
-        wait_recv(edge_copy(2, side), side)
-    planes(second_level, 0, RIM)
-    planes(second_level, cells - RIM, cells)
-
-    @pl.when(has_left)
-    def _():
-        planes(second_level, -RIM, 0)
-
-    @pl.when(has_right)
-    def _():
-        planes(second_level, cells, cells + RIM)
-
+        start(second_copy(half, 0), 0)
     def split(value, pieces):
         out = []
         for _ in range(pieces):
@@ -342,15 +322,42 @@
     for which in range(count):
         for a in range(3):
             for b in range(3):
-                for c in range(3):
-                    line = ((a * 3 + c) * 3 + b) * 16 + which
-                    tall[line : line + 1] = conv_in[which, a, b, c : c + 1]
+                line = (a * 9 + b) * 16 + which
+                tall[pl.ds(line, 3, stride=48)] = conv_in[which, a, b]
     line = 13 * 16 + count
     bias = bias_ref[...]
     tall[line : line + 1] = bias.astype(jnp.bfloat16).astype(jnp.float32)
     tall[line + 1 : line + 2] = bias - bias.astype(jnp.bfloat16).astype(jnp.float32)
     matrix_high, matrix_low = split(tall[...].T, 2)
     matrix_both = jnp.concatenate([matrix_high, matrix_low], axis=0)
+
+    lanes = coarse_x * coarse_z
+    summed[1] = jnp.zeros(summed.shape[1:], jnp.float32)
+    summed[1, :, count : count + 2] = jnp.ones((window, 2, lanes), jnp.float32)
+
+    @pl.when(jnp.logical_not(has_left))
+    def _():
+        summed[0] = jnp.zeros(summed.shape[1:], jnp.float32)
+
+    @pl.when(jnp.logical_not(has_right))
+    def _():
+        summed[2] = jnp.zeros(summed.shape[1:], jnp.float32)
+
+    for side in range(2):
+        wait_recv(first_copy(side, 1), side)
+    planes(second_level, 0, RIM)
+    planes(second_level, cells - RIM, cells)
+    for side in range(2):
+        wait_recv(first_copy(side, 0), side)
+        wait_recv(edge_copy(2, side), side)
+
+    @pl.when(has_left)
+    def _():
+        planes(second_level, -RIM, 0)
+
+    @pl.when(has_right)
+    def _():
+        planes(second_level, cells, cells + RIM)
 
     def products(level, rows_here, first):
         def body(which, carry):
@@ -369,7 +376,6 @@
 
         lax.fori_loop(0, count, body, 0)
 
-    lanes = coarse_x * coarse_z
     deep = coarse_x * size_z
     z_row = lax.broadcasted_iota(jnp.int32, (deep, lanes), 0)
     z_col = lax.broadcasted_iota(jnp.int32, (deep, lanes), 1)
@@ -413,15 +419,23 @@
                 row_copy(me_shot, target).start()
 
     products(first_lev, slice(0, size_y), True)
+    for kind, side in edges:
+        wait_send(edge_copy(kind, side), side)
+    for side in range(2):
+        for part in range(2):
+            wait_send(first_copy(side, part), side)
     sent = 0
     for half in range(HALVES):
-        for field, side in both:
-            wait_recv(second_copy(half, field, side), side)
+        for side in range(2):
+            wait_recv(second_copy(half, side), side)
         products(second[half], slice(half * half_y, (half + 1) * half_y), False)
         means(half)
         done = shots if half == HALVES - 1 else ((half + 1) * half_rows + 1 - window) // own_rows + 1
         send_rows(range(sent, done))
         sent = done
+    for half in range(HALVES):
+        for side in range(2):
+            wait_send(second_copy(half, side), side)
     parts[me_shot] = rows[pl.ds(me_shot * own_rows, window)]
     total = None
     for source in range(shots):
@@ -431,9 +445,7 @@
             row_copy(source, source).wait_recv()
 
         total = parts[source] if total is None else total + parts[source]
-    summed[1] = jnp.zeros(summed.shape[1:], jnp.float32)
     summed[1, :, 0:count] = total
-    summed[1, :, count : count + 2] = jnp.ones((window, 2, lanes), jnp.float32)
 
     def rim_copy(side):
         return remote(
@@ -446,14 +458,11 @@
 
     for side in range(2):
         start(rim_copy(side), side)
-
-    @pl.when(jnp.logical_not(has_left))
-    def _():
-        summed[0] = jnp.zeros(summed.shape[1:], jnp.float32)
-
-    @pl.when(jnp.logical_not(has_right))
-    def _():
-        summed[2] = jnp.zeros(summed.shape[1:], jnp.float32)
+    for target in range(shots):
+
+        @pl.when(me_shot != target)
+        def _():
+            row_copy(me_shot, target).wait_send()
 
     for side in range(2):
         wait_recv(rim_copy(side), side)
@@ -491,19 +500,6 @@
             for y in range(own_rows)
         ]
         out_ref[pl.ds(x, channels, stride=coarse_x)] = jnp.concatenate(pieces, axis=1)
-
-    for kind, side in edges:
-        wait_send(edge_copy(kind, side), side)
-    for field, side in both:
-        for part in range(2):
-            wait_send(first_copy(field, side, part), side)
-        for half in range(HALVES):
-            wait_send(second_copy(half, field, side), side)
-    for target in range(shots):
-
-        @pl.when(me_shot != target)
-        def _():
-            row_copy(me_shot, target).wait_send()
 
     for side in range(2):
         wait_send(rim_copy(side), side)
@@ -560,14 +556,14 @@
             pltpu.SemaphoreType.DMA((6,)),
             pltpu.SemaphoreType.DMA((3, 2)),
             pltpu.SemaphoreType.DMA((3, 2)),
-            pltpu.SemaphoreType.DMA((2, 2, 2)),
-            pltpu.SemaphoreType.DMA((2, 2, 2)),
+            pltpu.SemaphoreType.DMA((2, 2)),
+            pltpu.SemaphoreType.DMA((2, 2)),
             pltpu.SemaphoreType.DMA((shots,)),
             pltpu.SemaphoreType.DMA((shots,)),
             pltpu.SemaphoreType.DMA((2,)),
             pltpu.SemaphoreType.DMA((2,)),
-            pltpu.SemaphoreType.DMA((HALVES, 2, 2)),
-            pltpu.SemaphoreType.DMA((HALVES, 2, 2)),
+            pltpu.SemaphoreType.DMA((HALVES, 2)),
+            pltpu.SemaphoreType.DMA((HALVES, 2)),
         ],
         compiler_params=pltpu.CompilerParams(
             collective_id=0, has_side_effects=True, vmem_limit_bytes=63 * 1024 * 1024

time: 27.1 us -> 26.9 us (level)
  no operation moved by 1% of the time
where the time goes in v6:
time: 26.9 us; the launch traced here: 26.6 us
  Pallas kernels  25.9 us (96%)
  local copies, waits for them, and re-layouts  0.66 us (2%)
    pallas_call x1, Pallas kernels, local(): pl.pallas_call(functools.partial(kernel, (shots, slabs, cells, size_y, si...  25.9 us
    unnamed x1, local copies, waits for them, and re-layouts  0.66 us

profile of v6, /device:TPU:25, one launch (start us, length us, event | category | flops | bytes accessed | tf_op | source)
XLA Modules:
  0.0 26.6 jit_solution(18186086527718996189)
XLA Ops:
  0.0 25.9 %shard_map.118 = f32[256,64]{1,0:T(8,128)S(1)} custom-call(f32[1,16,64,128]{3,2,1,0:T(8,128)} %sp_ref.1, f32[1,16,64,128]{3,2,1,0:T(8,128)} %sn_ref.1, f32[1,16,64,128]{3,2,1,0:T(8,128)} %rp_ref.1, f32[1,16,64,128]{3,2,1,0:T(8,128)} %rn_ref.1, f32[16,64,128]{2,1,0:T(8,128)} %courant_ref.1, s32[1,8]{1,0:T(1,128)} %scells_ref.1, f32[1,2,8]{2,1,0:T(2,128)} %wavelet_ref.1, ...), custom_call_target="tpu_custom_call" | custom-call | flops 1500000000 | bytes 3000000 | tf_op jit(solution)/shard_map/pallas_call | solution.py:534
  26.0 0.7 %copy.14 = f32[64,4,64]{2,1,0:T(4,128)} copy(f32[64,4,64]{2,1,0:T(4,128)S(1)} %bitcast.3) | data formatting | bytes 131072

commit v7 on v6

--- a/solution.py
+++ b/solution.py
@@ -287,12 +287,24 @@
 
         lax.fori_loop(first, last, body, 0, unroll=True)
 
+    far_right = me_gx % 2 == 1
+
+    def sides_in_order(one, first_plane, size, copies):
+        for turn in range(2):
+            to_right = far_right if turn == 0 else jnp.logical_not(far_right)
+            base = jnp.where(to_right, first_plane[1], first_plane[0])
+            planes(lambda x: one(base + x), 0, size)
+            for side in range(2):
+                here = to_right if side == 1 else jnp.logical_not(to_right)
+
+                @pl.when(jnp.logical_and(here, goes(side)))
+                def _():
+                    for copy in copies(side):
+                        copy.start()
+
     for load in loads:
         load.wait()
-    planes(first_level, cells - H, cells - 1)
-    start(first_copy(1, 0), 1)
-    planes(first_level, 1, cells - H)
-    start(first_copy(0, 0), 0)
+    sides_in_order(first_level, (1, cells - H), H - 1, lambda side: [first_copy(side, 0)])
     for field, side in both:
         wait_recv(edge_copy(field, side), side)
     first_level(0)
@@ -301,12 +313,12 @@
         start(first_copy(side, 1), side)
 
     injection(1)
-    planes(second_level, cells - H, cells - RIM)
-    for half in range(HALVES):
-        start(second_copy(half, 1), 1)
-    planes(second_level, RIM, cells - H)
-    for half in range(HALVES):
-        start(second_copy(half, 0), 0)
+    sides_in_order(
+        second_level,
+        (RIM, cells - H),
+        H - RIM,
+        lambda side: [second_copy(half, side) for half in range(HALVES)],
+    )
     def split(value, pieces):
         out = []
         for _ in range(pieces):

time: 26.9 us -> 26.9 us (level)
  no operation moved by 1% of the time
where the time goes in v7:
time: 26.9 us; the launch traced here: 26.6 us
  Pallas kernels  25.9 us (96%)
  local copies, waits for them, and re-layouts  0.66 us (2%)
    pallas_call x1, Pallas kernels, local(): pl.pallas_call(functools.partial(kernel, (shots, slabs, cells, size_y, si...  25.9 us
    unnamed x1, local copies, waits for them, and re-layouts  0.66 us

profile of v7, /device:TPU:25, one launch (start us, length us, event | category | flops | bytes accessed | tf_op | source)
XLA Modules:
  0.0 26.6 jit_solution(9128224415193558089)
XLA Ops:
  0.0 25.9 %shard_map.118 = f32[256,64]{1,0:T(8,128)S(1)} custom-call(f32[1,16,64,128]{3,2,1,0:T(8,128)} %sp_ref.1, f32[1,16,64,128]{3,2,1,0:T(8,128)} %sn_ref.1, f32[1,16,64,128]{3,2,1,0:T(8,128)} %rp_ref.1, f32[1,16,64,128]{3,2,1,0:T(8,128)} %rn_ref.1, f32[16,64,128]{2,1,0:T(8,128)} %courant_ref.1, s32[1,8]{1,0:T(1,128)} %scells_ref.1, f32[1,2,8]{2,1,0:T(2,128)} %wavelet_ref.1, ...), custom_call_target="tpu_custom_call" | custom-call | flops 1500000000 | bytes 3000000 | tf_op jit(solution)/shard_map/pallas_call | solution.py:546
  26.0 0.7 %copy.14 = f32[64,4,64]{2,1,0:T(4,128)} copy(f32[64,4,64]{2,1,0:T(4,128)S(1)} %bitcast.3) | data formatting | bytes 131072
